TPU v7x, 256 devices: a whole 4x4x8 slice. The times are simulated.
256 devices in a mesh: dp: 16 (over z, y_lo), mp: 16 (over y_hi, x, core).
Axes of the slice: x: 4, y: 4 (y_hi: 2, y_lo: 2; y = y_hi * 2 + y_lo), z: 8, core: 2. Of those that a mesh axis runs over, the one named last changes fastest.
Arguments:
- grad_out: bfloat16 [16, 2048, 4096], P('dp', 'mp'), may hold values from -0.375 to 0.375
- hidden: bfloat16 [16, 2048, 14336], P('dp', None, 'mp'), may hold values from -6 to 6
- error: bfloat16 [16, 14336, 4096], P('dp', 'mp'), may hold values from -18 to 18
- q_prev: bfloat16 [4096, 64], replicated, may hold values from -6 to 6
Outputs:
- p_factor: bfloat16 [14336, 64], P('mp')
- q_factor: bfloat16 [4096, 64], replicated
All inputs are finite; a program needn't handle non-finite values.
Results may differ from a plain program's by a relative error of at most 0.005.
Values may be sent and summed in bfloat16 or wider, within the bound.
No kernel may reach another device: no remote copies, remote signals or barrier semaphores. Data moves between devices by JAX's collectives and lax.ppermute only.
A program may use at most 64 MiB of HBM per device.

v0:
```python
import math

import jax
import jax.numpy as jnp
from jax import lax
from jax.sharding import PartitionSpec as P

FF = 14336


def contract_rows(left, right):
    return lax.dot_general(
        left, right, (((0,), (0,)), ((), ())), preferred_element_type=jnp.float32
    )


def contract_high(left, right):
    return lax.dot_general(
        left,
        right,
        (((0,), (0,)), ((), ())),
        precision=lax.Precision.HIGHEST,
        preferred_element_type=jnp.float32,
    )


def on_device(grad_out, hidden, error, q_prev):
    g_rows = grad_out[0]
    h_rows = hidden[0]
    e_rows = error[0]
    proj_local = jnp.dot(g_rows, q_prev, preferred_element_type=jnp.float32).astype(jnp.bfloat16)
    base = jnp.dot(e_rows, q_prev, preferred_element_type=jnp.float32)
    block = h_rows
    p_local = base + contract_rows(block, lax.all_gather(proj_local, "mp", axis=0, tiled=True))
    p_sum = lax.psum(p_local, "dp")
    width = p_sum.shape[1] // 4
    done = []
    for number in range(4):
        columns = p_sum[:, number * width : (number + 1) * width]
        if number > 0:
            before = jnp.concatenate(done, axis=1)
            weights = lax.psum(contract_high(before, columns), "mp")
            columns = columns - jnp.dot(before, weights, precision=lax.Precision.HIGHEST)
        inner = lax.psum(contract_high(columns, columns), "mp")
        lower_factor = jnp.linalg.cholesky(inner)
        done.append(
            lax.linalg.triangular_solve(
                lower_factor, columns, left_side=False, lower=True, transpose_a=True
            )
        )
    orth = jnp.concatenate(done, axis=1)
    orth_b = orth.astype(jnp.bfloat16)
    block = h_rows
    mixed = lax.psum_scatter(
        jnp.dot(block, orth_b, preferred_element_type=jnp.float32),
        "mp",
        scatter_dimension=0,
        tiled=True,
    ).astype(jnp.bfloat16)
    q_local = contract_rows(g_rows, mixed) + contract_rows(e_rows, orth_b)
    groups = lax.axis_size("dp")
    q_factor = (lax.psum(q_local, ("dp", "mp")) / groups).astype(jnp.bfloat16)
    p_factor = (orth * math.sqrt(FF)).astype(jnp.bfloat16)
    return (p_factor, q_factor)


def solution(mesh):
    placed = (P("dp", "mp", None), P("dp", None, "mp"), P("dp", "mp", None), P())
    return jax.shard_map(
        on_device, mesh=mesh, in_specs=placed, out_specs=(P("mp", None), P()), check_vma=False
    )
```

profile of v0, /device:TPU:1, one launch (start us, length us, event | category | flops | bytes accessed | tf_op | source)
XLA Modules:
  0.0 843.8 jit_solution(16413270174528083460)
XLA Ops:
  7.2 0.0 copy-start
  7.2 0.0 all-reduce.3.cloned.1.call-start
  7.2 1.2 copy-done
  8.4 0.0 copy-start.1
  8.4 1.6 convolution_convert_fusion
  10.0 5.6 fusion.2
  15.6 27.1 %all_gather.3 = bf16[2048,64]{1,0:T(8,128)(2,1)S(1)} all-gather(bf16[128,64]{1,0:T(8,128)(2,1)S(1)} %convolution_convert_fusion), channel_id=1, replica_groups=mesh['dp'=16,'mp'=16] {'mp'}, dimensions={0}, use_global_device_ids=true | all-gather | bytes 278528 | tf_op jit(solution)/shard_map/all_gather | solution.py:34
  42.7 0.0 copy-done.1
  42.7 1.4 fusion.15
  44.1 0.0 all-reduce.3.cloned.1.call-update
  44.2 0.0 reduce-scatter.2.cloned.1.call-start
  44.2 122.7 %all-reduce.3.cloned.1.call-done = f32[896,64]{0,1:T(8,128)} async-done(((f32[896,64]{0,1:T(8,128)}), f32[896,64]{0,1:T(8,128)}) %all-reduce.3.cloned.1.call-update) | async-done | bytes 229392 | tf_op jit(solution)/shard_map/psum | solution.py:35
  166.9 1.1 fusion.28
  168.0 44.1 %psum.64 = f32[16,16]{0,1:T(8,128)S(1)} all-reduce(f32[16,16]{0,1:T(8,128)S(1)} %fusion.28), channel_id=1, replica_groups=mesh['dp'=16,'mp'=16] {'mp'}, use_global_device_ids=true, to_apply=%region_1.0 | all-reduce | flops 256 | bytes 2048 | tf_op jit(solution)/shard_map/psum | solution.py:44
  212.1 0.1 copy.7
  212.2 1.5 cholesky.74
  213.7 0.6 compare_reduce_fusion.3
  214.3 0.6 fusion.31
  215.0 1.2 custom-call.8
  216.2 1.1 convolution_bitcast_fusion.3
  217.3 1.0 fusion.25
  218.3 33.7 %psum.65 = f32[16,16]{1,0:T(8,128)S(1)} all-reduce(f32[16,16]{1,0:T(8,128)S(1)} %fusion.25), channel_id=1, replica_groups=mesh['dp'=16,'mp'=16] {'mp'}, use_global_device_ids=true, to_apply=%region_4.7 | all-reduce | flops 256 | bytes 2048 | tf_op jit(solution)/shard_map/psum | solution.py:42
  252.0 1.1 convolution_subtract_fusion.2
  253.0 0.2 fusion.49
  253.2 33.7 %psum.66 = f32[16,16]{0,1:T(8,128)S(1)} all-reduce(f32[16,16]{0,1:T(8,128)S(1)} %fusion.49), channel_id=1, replica_groups=mesh['dp'=16,'mp'=16] {'mp'}, use_global_device_ids=true, to_apply=%region_5.8 | all-reduce | flops 256 | bytes 2048 | tf_op jit(solution)/shard_map/psum | solution.py:44
  286.9 0.1 copy.9
  287.0 1.5 cholesky.85
  288.5 0.6 compare_reduce_fusion.2
  289.1 0.6 fusion.32
  289.8 1.2 custom-call.9
  291.0 0.3 convolution_bitcast_fusion.2
  291.3 1.0 fusion.22
  292.3 59.7 %psum.67 = f32[32,16]{1,0:T(8,128)S(1)} all-reduce(f32[32,16]{1,0:T(8,128)S(1)} %fusion.22), channel_id=1, replica_groups=mesh['dp'=16,'mp'=16] {'mp'}, use_global_device_ids=true, to_apply=%region_6.9 | all-reduce | flops 512 | bytes 4096 | tf_op jit(solution)/shard_map/psum | solution.py:42
  352.0 1.1 convolution_subtract_fusion.1
  353.1 0.2 fusion.50
  353.3 38.9 %psum.68 = f32[16,16]{0,1:T(8,128)S(1)} all-reduce(f32[16,16]{0,1:T(8,128)S(1)} %fusion.50), channel_id=1, replica_groups=mesh['dp'=16,'mp'=16] {'mp'}, use_global_device_ids=true, to_apply=%region_7.10 | all-reduce | flops 256 | bytes 2048 | tf_op jit(solution)/shard_map/psum | solution.py:44
  392.2 0.1 copy.11
  392.3 1.5 cholesky.96
  393.8 0.6 compare_reduce_fusion.1
  394.4 0.6 fusion.33
  395.1 1.2 custom-call.10
  396.3 0.3 convolution_bitcast_fusion.1
  396.5 1.1 fusion.21
  397.6 59.7 %psum.69 = f32[48,16]{1,0:T(8,128)S(1)} all-reduce(f32[48,16]{1,0:T(8,128)S(1)} %fusion.21), channel_id=1, replica_groups=mesh['dp'=16,'mp'=16] {'mp'}, use_global_device_ids=true, to_apply=%region_8.11 | all-reduce | flops 768 | bytes 6144 | tf_op jit(solution)/shard_map/psum | solution.py:42
  457.3 1.1 convolution_subtract_fusion
  458.4 0.2 fusion.51
  458.6 38.9 %psum.70 = f32[16,16]{0,1:T(8,128)S(1)} all-reduce(f32[16,16]{0,1:T(8,128)S(1)} %fusion.51), channel_id=1, replica_groups=mesh['dp'=16,'mp'=16] {'mp'}, use_global_device_ids=true, to_apply=%region_9.12 | all-reduce | flops 256 | bytes 2048 | tf_op jit(solution)/shard_map/psum | solution.py:44
  497.5 0.1 copy.13
  497.6 1.5 cholesky.107
  499.1 0.6 compare_reduce_fusion
  499.8 0.6 fusion.34
  500.4 1.2 custom-call.11
  501.6 0.3 convolution_bitcast_fusion
  501.9 4.1 fusion.9
  506.0 0.0 reduce-scatter.2.cloned.1.call-update
  506.0 0.0 all-reduce.5.cloned.1.call-start
  506.1 4.5 fusion
  510.6 63.7 %reduce-scatter.2.cloned.1.call-done = f32[128,64]{0,1:T(8,128)} async-done(((f32[2048,64]{0,1:T(8,128)}), f32[128,64]{0,1:T(8,128)}) %reduce-scatter.2.cloned.1.call-update) | async-done | bytes 32784 | tf_op jit(solution)/shard_map/reduce_scatter | solution.py:54
  574.2 2.0 fusion.4
  576.3 0.0 all-reduce.5.cloned.1.call-update
  576.3 0.7 multiply_convert_fusion.1
  577.0 258.3 %all-reduce.5.cloned.1.call-done = f32[4096,64]{0,1:T(8,128)} async-done(((f32[4096,64]{0,1:T(8,128)}), f32[4096,64]{0,1:T(8,128)}) %all-reduce.5.cloned.1.call-update) | async-done | bytes 1048592 | tf_op jit(solution)/shard_map/psum | solution.py:62
  835.2 2.1 multiply_convert_fusion
  (8 shorter events, 0.2 us)
Async XLA Ops:
  7.2 1.2 copy-start
  7.2 159.7 %all-reduce.3.cloned.1.call-start = ((), (), s32[]{:S(2)}) async-start(), calls=%async_computation.1 | async-start | bytes 458752 | tf_op jit(solution)/shard_map/psum | solution.py:35
  8.4 34.3 %copy-start.1 = (bf16[1,2048,896]{2,1,0:T(8,128)(2,1)S(1)}, bf16[1,2048,896]{2,1,0:T(8,128)(2,1)}, u32[]{:S(2)}) copy-start(bf16[1,2048,896]{2,1,0:T(8,128)(2,1)} %param.8) | copy-start | bytes 11010052
  44.2 530.1 %reduce-scatter.2.cloned.1.call-start = ((), (), s32[]{:S(2)}) async-start(), calls=%async_computation.2 | async-start | bytes 557056 | tf_op jit(solution)/shard_map/reduce_scatter | solution.py:54
  506.0 329.2 %all-reduce.5.cloned.1.call-start = ((), (), s32[]{:S(2)}) async-start(), calls=%async_computation.3 | async-start | bytes 2097152 | tf_op jit(solution)/shard_map/psum | solution.py:62
Sparse Core Ops, SparseCore 0:
  44.3 122.5 all-reduce.2
  506.1 68.0 reduce-scatter.1
  579.7 255.5 all-reduce.4
where the time goes:
time: 845 us; the launch traced here: 844 us
  waiting for transfers between devices  445 us (53%)
  blocking collectives  336 us (40%)
  matrix products  29.1 us (3%)
  other arithmetic  18.8 us (2%)
  between operations  13.9 us (2%)
    psum x1, waiting for transfers between devices, on_device(): q_factor = (lax.psum(q_local, ('dp', 'mp')) / groups).astype(jnp.bfloat16)  258 us
    psum x4, blocking collectives, on_device(): inner = lax.psum(contract_high(columns, columns), 'mp')  156 us
    psum x3, blocking collectives, on_device(): weights = lax.psum(contract_high(before, columns), 'mp')  153 us
    psum x1, waiting for transfers between devices, on_device(): p_sum = lax.psum(p_local, 'dp')  123 us
    reduce_scatter x1, waiting for transfers between devices, on_device(): lax.psum_scatter(jnp.dot(block, orth_b, preferred_element_type=jnp.float3...  63.7 us
    all_gather x1, blocking collectives, on_device(): lax.all_gather(proj_local, 'mp', axis=0, tiled=True)  27.1 us
  transfers between devices with their start and end apart: 3, of which 3 were waited for; matrix products, arithmetic and copies ran while one was open for 1% of the time, Pallas kernels for 0%

commit v1 on v0

v1 whole, which is shorter than its diff:
```python
import math

import jax
import jax.numpy as jnp
from jax import lax
from jax.experimental import pallas as pl
from jax.experimental.pallas import tpu as pltpu
from jax.sharding import Mesh
from jax.sharding import PartitionSpec as P

FF = 14336
AXES = ("z", "ylo", "yhi", "x", "core")
SIZES = (-1, 2, 2, 4, 2)
DP = ("z", "ylo")
MP = ("yhi", "x", "core")
PLANE = ("ylo", "yhi", "x")


def contract(left, right, dims):
    return lax.dot_general(left, right, (dims, ((), ())), preferred_element_type=jnp.float32)


def exchange(parts, axis):
    return lax.all_to_all(parts, axis, split_axis=0, concat_axis=0, tiled=True)


def spread(block, axis):
    size = lax.axis_size(axis)
    return exchange(jnp.broadcast_to(block[None], (size,) + block.shape), axis)


def swap(block):
    return lax.ppermute(block, "core", [(0, 1), (1, 0)])


def total(parts):
    return jnp.sum(parts.astype(jnp.float32), axis=0)


def halves(array):
    high = lax.reduce_precision(array, 8, 7)
    return high.astype(jnp.bfloat16), (array - high).astype(jnp.bfloat16)


def whole(pair):
    width = pair.shape[1] // 2
    return pair[:, :width] + pair[:, width:]


def by_lanes(array, count):
    return array.reshape(array.shape[0], count, -1).transpose(1, 0, 2)


def eliminate(parts_ref, inverse_ref, pair_ref):
    rank = inverse_ref.shape[0]
    gram = [parts_ref[j][rank:].astype(jnp.float32) for j in range(rank // 8)]
    gram = jnp.concatenate(gram, axis=0)
    gram = gram[:, :rank] + gram[:, rank:]
    row_at = lax.broadcasted_iota(jnp.int32, gram.shape, 0)
    column_at = lax.broadcasted_iota(jnp.int32, gram.shape, 1)
    start = jnp.concatenate([gram, (row_at == column_at).astype(jnp.float32)], axis=1)
    rows = [start[8 * b : 8 * b + 8, :] for b in range(rank // 8)]
    place = lax.broadcasted_iota(jnp.int32, (8, 1), 0)
    for k in range(0, rank, 2):
        at, inner = divmod(k, 8)
        one, two = rows[at][inner : inner + 1, :], rows[at][inner + 1 : inner + 2, :]
        pivot = jnp.broadcast_to(one[:, k : k + 1], one.shape)
        beside = jnp.broadcast_to(one[:, k + 1 : k + 2], one.shape)
        below = jnp.broadcast_to(two[:, k + 1 : k + 2], one.shape)
        scale = lax.rsqrt(pivot)
        inverse_ref[k : k + 1, :] = (one * scale)[:, rank:]
        unit = scale * scale
        ratio = beside * unit
        two = two - ratio * one
        scale = lax.rsqrt(below - ratio * beside)
        inverse_ref[k + 1 : k + 2, :] = (two * scale)[:, rank:]
        two = two * (scale * scale)
        one = one * unit - ratio * two
        for b in range(at, rank // 8):
            left = rows[b] - rows[b][:, k : k + 1] * one - rows[b][:, k + 1 : k + 2] * two
            rows[b] = jnp.where(place > inner + 1, left, rows[b]) if b == at else left
    inverse = inverse_ref[...] * math.sqrt(FF)
    high = inverse.astype(jnp.bfloat16)
    low = inverse - high.astype(jnp.float32)
    pair_ref[...] = jnp.concatenate([high, low.astype(jnp.bfloat16)], axis=1)


def inverse_factor(parts, rank):
    return pl.pallas_call(
        eliminate,
        out_shape=[
            jax.ShapeDtypeStruct((rank, rank), jnp.float32),
            jax.ShapeDtypeStruct((rank, 2 * rank), jnp.bfloat16),
        ],
        in_specs=[pl.BlockSpec(memory_space=pltpu.VMEM)],
        out_specs=[pl.BlockSpec(memory_space=pltpu.VMEM)] * 2,
        cost_estimate=pl.CostEstimate(flops=4_000_000_000, bytes_accessed=49152, transcendentals=64),
        name="inverse_factor",
    )(parts)


def on_device(grad_out, hidden, error, q_prev):
    bf16, f32 = jnp.bfloat16, jnp.float32
    g_rows, h_rows, e_rows = grad_out[0], hidden[0], error[0]
    groups, parts, plane = lax.axis_size(DP), lax.axis_size(MP), lax.axis_size(PLANE)
    rank = q_prev.shape[1]
    units = h_rows.shape[1]
    some = rank // parts

    proj_local = jnp.dot(g_rows, q_prev, preferred_element_type=f32).astype(bf16)
    first, proj_local = lax.optimization_barrier((lax.axis_index("core") == 0, proj_local))
    proj = spread(proj_local, MP).reshape(h_rows.shape[0], rank)
    base = jnp.dot(e_rows, q_prev, preferred_element_type=f32)
    p_local = base + contract(h_rows, proj, ((0,), (0,)))
    p_terms = p_local.astype(bf16).reshape(groups, units // groups, rank)
    p_part = total(exchange(p_terms, DP)).astype(bf16)
    p_sum = spread(p_part, DP).reshape(units, rank)

    gram_terms = jnp.concatenate(halves(contract(p_sum, p_sum, ((0,), (0,)))), axis=1)
    gram_terms = jnp.pad(gram_terms.reshape(parts, some, -1), ((0, 0), (0, 8 - some), (0, 0)))
    mixed_terms = by_lanes(contract(p_sum, h_rows, ((0,), (1,))).astype(bf16), parts)
    got = exchange(jnp.concatenate([mixed_terms, gram_terms], axis=1), MP)
    mixed = total(got[:, :rank]).astype(bf16)
    gram_rows = jnp.concatenate(halves(whole(total(got[:, rank : rank + some]))), axis=1)

    q_local = contract(p_sum, e_rows, ((0,), (0,))) + contract(mixed, g_rows, ((1,), (0,)))
    half = q_local.shape[1] // 2
    left, right = q_local[:, :half], q_local[:, half:]
    other = swap(jnp.where(first, right, left).astype(bf16))
    other_rows = swap(gram_rows)
    gram_rows = jnp.concatenate(
        [jnp.where(first, gram_rows, other_rows), jnp.where(first, other_rows, gram_rows)]
    )
    q_pair = (jnp.where(first, left, right) + other.astype(f32)).astype(bf16)
    gram_rows = jnp.broadcast_to(gram_rows[None], (plane,) + gram_rows.shape)
    got = exchange(jnp.concatenate([by_lanes(q_pair, plane), gram_rows], axis=1), PLANE)
    q_share = total(got[:, :rank]).astype(bf16)
    q_share, got = lax.optimization_barrier((q_share, got))
    inverse, pair = inverse_factor(got, rank)
    q_share = total(spread(q_share, "z"))
    q_share = jnp.dot(inverse / groups, q_share, precision=lax.Precision.HIGHEST).astype(bf16)
    mine = spread(q_share, PLANE).transpose(1, 0, 2).reshape(rank, -1)
    other = swap(mine)
    q_factor = jnp.concatenate(
        [jnp.where(first, mine, other), jnp.where(first, other, mine)], axis=1
    ).T
    twice = jnp.concatenate([p_sum, p_sum], axis=1)
    p_factor = contract(twice, pair, ((1,), (1,))).astype(bf16)
    return (p_factor, q_factor)


def solution(mesh):
    by_chip = Mesh(mesh.devices.reshape(SIZES), AXES)
    placed = (P(DP, MP, None), P(DP, None, MP), P(DP, MP, None), P())
    return jax.shard_map(
        on_device, mesh=by_chip, in_specs=placed, out_specs=(P(MP, None), P()), check_vma=False
    )
```

time: 845 us -> 118 us (0.14)
  waiting for transfers between devices: 445 us -> 11.2 us
  blocking collectives: 336 us -> 49.3 us
  starting transfers between devices: 0.12 us -> 23.8 us
  other arithmetic: 18.8 us -> 2.34 us
  between operations: 13.9 us -> 0.83 us
    psum x2 -> x0, waiting for transfers between devices: 381 us -> none  [the longest x1 258 us: on_device(): q_factor = (lax.psum(q_local, ('dp', 'mp')) / groups).astype(jnp.bfloat16)]
    psum x7 -> x0, blocking collectives: 309 us -> none  [the longest x4 156 us: on_device(): inner = lax.psum(contract_high(columns, columns), 'mp')]
    reduce_scatter x1 -> x0, waiting for transfers between devices: 63.7 us -> none  [on_device(): lax.psum_scatter(jnp.dot(block, orth_b, preferred_element_type=jnp.float3...]
    all_to_all x0 -> x4, blocking collectives: none -> 49.3 us  [exchange(): return lax.all_to_all(parts, axis, split_axis=0, concat_axis=0, tiled=True)]
    all_gather x1 -> x0, blocking collectives: 27.1 us -> none  [on_device(): lax.all_gather(proj_local, 'mp', axis=0, tiled=True)]
    all_to_all x0 -> x3, starting transfers between devices: none -> 19.2 us  [exchange(): return lax.all_to_all(parts, axis, split_axis=0, concat_axis=0, tiled=True)]
    another operation x20 -> x0, other arithmetic: 16 us -> none  [the longest x12 8.52 us: on_device(): lower_factor = jnp.linalg.cholesky(inner)]
    all_to_all x0 -> x3, waiting for transfers between devices: none -> 9.79 us  [exchange(): return lax.all_to_all(parts, axis, split_axis=0, concat_axis=0, tiled=True)]
  transfers between devices with their start and end apart: 3 -> 6, of which waited for: 3 -> 5; matrix products, arithmetic and copies ran while one was open for 1% -> 10% of each run, Pallas kernels for 0% -> 5%
where the time goes in v1:
time: 118 us; the launch traced here: 117 us
  blocking collectives  49.3 us (42%)
  starting transfers between devices  23.8 us (20%)
  matrix products  20.8 us (18%)
  waiting for transfers between devices  11.2 us (9%)
  Pallas kernels  5.34 us (5%)
  local copies, waits for them, and re-layouts  3.74 us (3%)
  other arithmetic  2.34 us (2%)
    all_to_all x4, blocking collectives, exchange(): return lax.all_to_all(parts, axis, split_axis=0, concat_axis=0, tiled=True)  49.3 us
    all_to_all x3, starting transfers between devices, exchange(): return lax.all_to_all(parts, axis, split_axis=0, concat_axis=0, tiled=True)  19.2 us
    dot_general x6, matrix products, contract(): lax.dot_general(left, right, (dims, ((), ())), preferred_element_type=jnp...  12.7 us
    all_to_all x3, waiting for transfers between devices, exchange(): return lax.all_to_all(parts, axis, split_axis=0, concat_axis=0, tiled=True)  9.79 us
    dot_general x1, matrix products, on_device(): base = jnp.dot(e_rows, q_prev, preferred_element_type=f32)  5.6 us
    pallas_call x1, Pallas kernels, inverse_factor(): pl.pallas_call(eliminate, out_shape=[jax.ShapeDtypeStruct((rank, rank), j...  5.34 us
    ppermute x3, starting transfers between devices, swap(): return lax.ppermute(block, 'core', [(0, 1), (1, 0)])  4.59 us
  transfers between devices with their start and end apart: 6, of which 5 were waited for; matrix products, arithmetic and copies ran while one was open for 10% of the time, Pallas kernels for 5%

profile of v1, /device:TPU:1, one launch (start us, length us, event | category | flops | bytes accessed | tf_op | source)
XLA Modules:
  0.0 117.4 jit_solution(689471518107441817)
XLA Ops:
  0.6 0.0 copy-start
  0.6 1.2 %copy-done = bf16[1,128,4096]{2,1,0:T(8,128)(2,1)S(1)} copy-done((bf16[1,128,4096]{2,1,0:T(8,128)(2,1)S(1)}, bf16[1,128,4096]{2,1,0:T(8,128)(2,1)}, u32[]{:S(2)}) %copy-start) | copy-done | bytes 1048600
  1.9 1.5 %convolution_convert_fusion.1 = bf16[128,64]{0,1:T(8,128)(2,1)S(1)} fusion(bf16[4096,64]{0,1:T(8,128)(2,1)} %param.7, bf16[1,128,4096]{2,1,0:T(8,128)(2,1)S(1)} %copy-done), kind=kOutput, calls=%fused_computation.16 | convolution fusion | flops 67117056 | bytes 1589248 | tf_op jit(solution)/shard_map/dot_general | solution.py:110
  3.4 0.8 broadcast_in_dim.10
  4.1 8.4 %all-to-all-start = ((bf16[16,128,64]{1,2,0:T(8,128)(2,1)}), bf16[16,128,64]{1,2,0:T(8,128)(2,1)S(1)}, u32[]{:S(2)}, u32[]{:S(2)}) async-start(bf16[16,128,64]{1,2,0:T(8,128)(2,1)} %broadcast_in_dim.10), calls=%async_computation | async-start | bytes 524288 | tf_op jit(solution)/shard_map/all_to_all | solution.py:24
  12.6 5.6 %fusion.2 = f32[896,64]{0,1:T(8,128)S(1)} fusion(bf16[4096,64]{0,1:T(8,128)(2,1)} %param.7, bf16[1,896,4096]{2,1,0:T(8,128)(2,1)} %param.6), kind=kOutput, calls=%fused_computation.2 | convolution fusion | flops 469762048 | bytes 8093696 | tf_op jit(solution)/shard_map/dot_general | solution.py:113
  18.2 3.1 %all-to-all-done = bf16[16,128,64]{1,2,0:T(8,128)(2,1)S(1)} async-done(((bf16[16,128,64]{1,2,0:T(8,128)(2,1)}), bf16[16,128,64]{1,2,0:T(8,128)(2,1)S(1)}, u32[]{:S(2)}, u32[]{:S(2)}) %all-to-all-start) | async-done | bytes 262176 | tf_op jit(solution)/shard_map/all_to_all | solution.py:24
  21.3 2.8 %fusion.20 = bf16[896,64]{0,1:T(8,128)(2,1)S(1)} fusion(f32[896,64]{0,1:T(8,128)S(1)} %fusion.2, bf16[1,2048,896]{2,1,0:T(8,128)(2,1)} %param.5, bf16[16,128,64]{1,2,0:T(8,128)(2,1)S(1)} %all-to-all-done), kind=kOutput, calls=%fused_computation.13 | convolution fusion | flops 234995712 | bytes 4276224 | tf_op jit(solution)/shard_map/dot_general | solution.py:20
  24.0 0.2 copy.31
  24.2 0.2 reshape.38
  24.4 16.6 %all_to_all.35 = bf16[16,2,1792]{2,1,0:T(2,128)(2,1)S(1)} all-to-all(bf16[16,2,1792]{2,1,0:T(2,128)(2,1)S(1)} %reshape.38), channel_id=1, replica_groups=mesh['z'=8,'ylo'=2,'yhi'=2,'x'=4,'core'=2] {'z','ylo'}, dimensions={0} | all-to-all | bytes 229376 | tf_op jit(solution)/shard_map/all_to_all | solution.py:24
  41.0 0.2 reshape.39
  41.2 0.1 reduce_sum.54
  41.3 0.2 reshape.40
  41.5 11.0 %all_to_all.36 = bf16[16,2,1792]{2,1,0:T(2,128)(2,1)S(1)} all-to-all(bf16[16,2,1792]{2,1,0:T(2,128)(2,1)S(1)} %reshape.40), channel_id=1, replica_groups=mesh['z'=8,'ylo'=2,'yhi'=2,'x'=4,'core'=2] {'z','ylo'}, dimensions={0} | all-to-all | bytes 229376 | tf_op jit(solution)/shard_map/all_to_all | solution.py:24
  52.5 0.2 reshape.41
  52.7 0.2 reduce-precision_convert_fusion
  52.9 3.3 %fusion.11 = bf16[8,16,8,128]{3,2,1,0:T(8,128)(2,1)S(1)} fusion(bf16[896,64]{1,0:T(8,128)(2,1)S(1)} %bitcast.81, bf16[1,2048,896]{2,1,0:T(8,128)(2,1)} %param.5), kind=kOutput, calls=%fused_computation.10 | convolution fusion | flops 235012096 | bytes 4046848 | tf_op jit(solution)/shard_map/dot_general | solution.py:20
  56.2 0.1 copy.48
  56.3 0.1 pad_maximum_fusion.1
  56.3 0.7 fusion.26
  57.1 7.4 %all-to-all-start.3 = ((bf16[16,72,128]{2,1,0:T(8,128)(2,1)}), bf16[16,72,128]{2,1,0:T(8,128)(2,1)S(1)}, u32[]{:S(2)}, u32[]{:S(2)}) async-start(bf16[16,72,128]{2,1,0:T(8,128)(2,1)} %fusion.26), calls=%async_computation.3 | async-start | bytes 589824 | tf_op jit(solution)/shard_map/all_to_all | solution.py:24
  64.5 4.5 %fusion = f32[64,4096]{1,0:T(8,128)S(1)} fusion(bf16[896,64]{1,0:T(8,128)(2,1)S(1)} %bitcast.82, bf16[1,896,4096]{2,1,0:T(8,128)(2,1)} %param.6), kind=kOutput, calls=%fused_computation | convolution fusion | flops 469762048 | bytes 8503296 | tf_op jit(solution)/shard_map/dot_general | solution.py:20
  69.0 4.4 %all-to-all-done.3 = bf16[16,72,128]{2,1,0:T(8,128)(2,1)S(1)} async-done(((bf16[16,72,128]{2,1,0:T(8,128)(2,1)}), bf16[16,72,128]{2,1,0:T(8,128)(2,1)S(1)}, u32[]{:S(2)}, u32[]{:S(2)}) %all-to-all-start.3) | async-done | bytes 294944 | tf_op jit(solution)/shard_map/all_to_all | solution.py:24
  73.4 0.1 reduce-precision_convert_fusion.1
  73.5 0.1 pad_maximum_fusion.3
  73.6 0.9 collective-permute-start.1
  74.5 0.3 convolution_add_fusion
  74.8 0.1 select_convert_fusion
  74.9 0.1 collective-permute-start
  75.0 0.3 collective-permute-done.1
  75.3 0.1 broadcast_select_fusion.3
  75.4 1.1 collective-permute-done
  76.5 0.1 bitcast_bitcast_fusion
  76.7 11.6 %all_to_all.37.parts_ref = bf16[16,72,128]{2,1,0:T(8,128)(2,1)S(1)} all-to-all(bf16[16,72,128]{2,1,0:T(8,128)(2,1)S(1)} %pad_maximum_fusion), channel_id=1, replica_groups=mesh['z'=8,'ylo'=2,'yhi'=2,'x'=4,'core'=2] {'ylo','yhi','x'}, dimensions={0} | all-to-all | bytes 589824 | tf_op jit(solution)/shard_map/all_to_all | solution.py:24
  88.3 0.0 copy-start.1
  88.3 0.7 broadcast_in_dim.13
  89.0 3.4 %all-to-all-start.5 = ((bf16[8,64,128]{2,1,0:T(8,128)(2,1)}), bf16[8,64,128]{2,1,0:T(8,128)(2,1)S(1)}, u32[]{:S(2)}, u32[]{:S(2)}) async-start(bf16[8,64,128]{2,1,0:T(8,128)(2,1)} %broadcast_in_dim.13), calls=%async_computation.5 | async-start | bytes 262144 | tf_op jit(solution)/shard_map/all_to_all | solution.py:24
  92.4 0.0 copy-done.1
  92.4 5.3 %inverse_factor.1 = (f32[64,64]{1,0:T(8,128)}, bf16[64,128]{1,0:T(8,128)(2,1)}) custom-call(bf16[16,72,128]{2,1,0:T(8,128)(2,1)} %copy-done.1), custom_call_target="tpu_custom_call" | custom-call | flops 4000000000 | bytes 49152 | tf_op jit(solution)/shard_map/inverse_factor/pallas_call | solution.py:89
  97.7 2.3 %all-to-all-done.5 = bf16[8,64,128]{2,1,0:T(8,128)(2,1)S(1)} async-done(((bf16[8,64,128]{2,1,0:T(8,128)(2,1)}), bf16[8,64,128]{2,1,0:T(8,128)(2,1)S(1)}, u32[]{:S(2)}, u32[]{:S(2)}) %all-to-all-start.5) | async-done | bytes 131104 | tf_op jit(solution)/shard_map/all_to_all | solution.py:24
  100.1 0.9 convolution_convert_fusion.2
  101.1 10.1 %all_to_all.38 = bf16[16,64,128]{2,1,0:T(8,128)(2,1)S(1)} all-to-all(bf16[16,64,128]{2,1,0:T(8,128)(2,1)S(1)} %broadcast_in_dim.14), channel_id=1, replica_groups=mesh['z'=8,'ylo'=2,'yhi'=2,'x'=4,'core'=2] {'ylo','yhi','x'}, dimensions={0} | all-to-all | bytes 524288 | tf_op jit(solution)/shard_map/all_to_all | solution.py:24
  111.2 3.6 %collective-permute-start.2 = (bf16[64,2048]{1,0:T(8,128)(2,1)S(1)}, bf16[64,2048]{1,0:T(8,128)(2,1)S(1)}, u32[]{:S(2)}, u32[]{:S(2)}) collective-permute-start(bf16[64,2048]{1,0:T(8,128)(2,1)S(1)} %copy_bitcast_fusion), channel_id=1, source_target_pairs={{0,1},{1,0},{2,3},{3,2},{4,5},{5,4},{6,7},{7,6},{8,9},{9,8},{10,11... | collective-permute-start | bytes 786440 | tf_op jit(solution)/shard_map/ppermute | solution.py:33
  114.8 1.6 %convolution_convert_fusion = bf16[896,64]{0,1:T(8,128)(2,1)} fusion(bf16[64,128]{1,0:T(8,128)(2,1)} %get-tuple-element.11, bf16[896,64]{1,0:T(8,128)(2,1)S(1)} %bitcast.83), kind=kOutput, calls=%fused_computation.14 | convolution fusion | flops 15196160 | bytes 245760 | tf_op jit(solution)/shard_map/dot_general | solution.py:20
  116.5 0.0 collective-permute-done.2
  116.5 0.1 broadcast_select_fusion.1
  116.6 0.8 maximum_bitcast_fusion
  (10 shorter events, 0.3 us)
Async XLA Ops:
  0.6 1.2 %copy-start = (bf16[1,128,4096]{2,1,0:T(8,128)(2,1)S(1)}, bf16[1,128,4096]{2,1,0:T(8,128)(2,1)}, u32[]{:S(2)}) copy-start(bf16[1,128,4096]{2,1,0:T(8,128)(2,1)} %param.4) | copy-start | bytes 3145732
  4.1 17.1 %all-to-all-start = ((bf16[16,128,64]{1,2,0:T(8,128)(2,1)}), bf16[16,128,64]{1,2,0:T(8,128)(2,1)S(1)}, u32[]{:S(2)}, u32[]{:S(2)}) async-start(bf16[16,128,64]{1,2,0:T(8,128)(2,1)} %broadcast_in_dim.10), calls=%async_computation | async-start | bytes 524288 | tf_op jit(solution)/shard_map/all_to_all | solution.py:24
  57.1 16.3 %all-to-all-start.3 = ((bf16[16,72,128]{2,1,0:T(8,128)(2,1)}), bf16[16,72,128]{2,1,0:T(8,128)(2,1)S(1)}, u32[]{:S(2)}, u32[]{:S(2)}) async-start(bf16[16,72,128]{2,1,0:T(8,128)(2,1)} %fusion.26), calls=%async_computation.3 | async-start | bytes 589824 | tf_op jit(solution)/shard_map/all_to_all | solution.py:24
  73.6 1.7 %collective-permute-start.1 = (bf16[4,128]{1,0:T(4,128)(2,1)S(1)}, bf16[4,128]{1,0:T(4,128)(2,1)S(1)}, u32[]{:S(2)}, u32[]{:S(2)}) collective-permute-start(bf16[4,128]{1,0:T(4,128)(2,1)S(1)} %pad_maximum_fusion.3), channel_id=1, source_target_pairs={{0,1},{1,0},{2,3},{3,2},{4,5},{5,4},{6,7},{7,6},{8,9},{9,8},{10,11... | collective-permute-start | bytes 3080 | tf_op jit(solution)/shard_map/ppermute | solution.py:33
  74.9 1.6 %collective-permute-start = (bf16[64,2048]{1,0:T(8,128)(2,1)S(1)}, bf16[64,2048]{1,0:T(8,128)(2,1)S(1)}, u32[]{:S(2)}, u32[]{:S(2)}) collective-permute-start(bf16[64,2048]{1,0:T(8,128)(2,1)S(1)} %select_convert_fusion), channel_id=1, source_target_pairs={{0,1},{1,0},{2,3},{3,2},{4,5},{5,4},{6,7},{7,6},{8,9},{9,8},{10,11... | collective-permute-start | bytes 786440 | tf_op jit(solution)/shard_map/ppermute | solution.py:33
  88.3 4.1 %copy-start.1 = (bf16[16,72,128]{2,1,0:T(8,128)(2,1)}, bf16[16,72,128]{2,1,0:T(8,128)(2,1)S(1)}, u32[]{:S(2)}) copy-start(bf16[16,72,128]{2,1,0:T(8,128)(2,1)S(1)} %all_to_all.37.parts_ref) | copy-start | bytes 884740
  89.0 11.1 %all-to-all-start.5 = ((bf16[8,64,128]{2,1,0:T(8,128)(2,1)}), bf16[8,64,128]{2,1,0:T(8,128)(2,1)S(1)}, u32[]{:S(2)}, u32[]{:S(2)}) async-start(bf16[8,64,128]{2,1,0:T(8,128)(2,1)} %broadcast_in_dim.13), calls=%async_computation.5 | async-start | bytes 262144 | tf_op jit(solution)/shard_map/all_to_all | solution.py:24
  111.2 5.2 %collective-permute-start.2 = (bf16[64,2048]{1,0:T(8,128)(2,1)S(1)}, bf16[64,2048]{1,0:T(8,128)(2,1)S(1)}, u32[]{:S(2)}, u32[]{:S(2)}) collective-permute-start(bf16[64,2048]{1,0:T(8,128)(2,1)S(1)} %copy_bitcast_fusion), channel_id=1, source_target_pairs={{0,1},{1,0},{2,3},{3,2},{4,5},{5,4},{6,7},{7,6},{8,9},{9,8},{10,11... | collective-permute-start | bytes 786440 | tf_op jit(solution)/shard_map/ppermute | solution.py:33

commit v2 on v1

--- a/solution.py
+++ b/solution.py
@@ -9,6 +9,8 @@
 from jax.sharding import PartitionSpec as P
 
 FF = 14336
+GROUPS = 16
+VMEM_BYTES = 4 << 20
 AXES = ("z", "ylo", "yhi", "x", "core")
 SIZES = (-1, 2, 2, 4, 2)
 DP = ("z", "ylo")
@@ -51,9 +53,11 @@
     return array.reshape(array.shape[0], count, -1).transpose(1, 0, 2)
 
 
-def eliminate(parts_ref, inverse_ref, pair_ref):
+def eliminate(zero_ref, one_ref, q_pair_ref, p_pair_ref, inverse_ref):
     rank = inverse_ref.shape[0]
-    gram = [parts_ref[j][rank:].astype(jnp.float32) for j in range(rank // 8)]
+    gram = []
+    for j in range(rank // 8):
+        gram += [ref[j].astype(jnp.float32)[:4] for ref in (zero_ref, one_ref)]
     gram = jnp.concatenate(gram, axis=0)
     gram = gram[:, :rank] + gram[:, rank:]
     row_at = lax.broadcasted_iota(jnp.int32, gram.shape, 0)
@@ -79,24 +83,56 @@
         for b in range(at, rank // 8):
             left = rows[b] - rows[b][:, k : k + 1] * one - rows[b][:, k + 1 : k + 2] * two
             rows[b] = jnp.where(place > inner + 1, left, rows[b]) if b == at else left
-    inverse = inverse_ref[...] * math.sqrt(FF)
-    high = inverse.astype(jnp.bfloat16)
-    low = inverse - high.astype(jnp.float32)
-    pair_ref[...] = jnp.concatenate([high, low.astype(jnp.bfloat16)], axis=1)
+    inverse = inverse_ref[...]
+    q_pair_ref[...] = halves_in(inverse * (1.0 / GROUPS))
+    p_pair_ref[...] = halves_in(inverse * math.sqrt(FF))
 
 
-def inverse_factor(parts, rank):
+def halves_in(array):
+    high = array.astype(jnp.bfloat16)
+    low = (array - high.astype(jnp.float32)).astype(jnp.bfloat16)
+    return jnp.concatenate([high, low], axis=1)
+
+
+def inverse_factor(zero, one, rank):
+    pair = jax.ShapeDtypeStruct((rank, 2 * rank), jnp.bfloat16)
     return pl.pallas_call(
         eliminate,
-        out_shape=[
-            jax.ShapeDtypeStruct((rank, rank), jnp.float32),
-            jax.ShapeDtypeStruct((rank, 2 * rank), jnp.bfloat16),
-        ],
-        in_specs=[pl.BlockSpec(memory_space=pltpu.VMEM)],
+        out_shape=[pair, pair],
+        in_specs=[pl.BlockSpec(memory_space=pltpu.VMEM)] * 2,
         out_specs=[pl.BlockSpec(memory_space=pltpu.VMEM)] * 2,
+        scratch_shapes=[pltpu.VMEM((rank, rank), jnp.float32)],
         cost_estimate=pl.CostEstimate(flops=4_000_000_000, bytes_accessed=49152, transcendentals=64),
+        compiler_params=pltpu.CompilerParams(vmem_limit_bytes=VMEM_BYTES),
         name="inverse_factor",
-    )(parts)
+    )(zero, one)
+
+
+def scale_share(parts_ref, pair_ref, out_ref):
+    rank = pair_ref.shape[0]
+    share = parts_ref[0].astype(jnp.float32)
+    for j in range(1, parts_ref.shape[0]):
+        share = share + parts_ref[j].astype(jnp.float32)
+    high = share.astype(jnp.bfloat16)
+    low = (share - high.astype(jnp.float32)).astype(jnp.bfloat16)
+    pair = pair_ref[...]
+    scaled = contract(pair, jnp.concatenate([high, high], axis=0), ((1,), (0,)))
+    scaled = scaled + contract(pair[:, :rank], low, ((1,), (0,)))
+    scaled = scaled.astype(jnp.bfloat16)
+    for j in range(out_ref.shape[0]):
+        out_ref[j] = scaled
+
+
+def scaled_copies(parts, pair, count):
+    return pl.pallas_call(
+        scale_share,
+        out_shape=jax.ShapeDtypeStruct((count,) + parts.shape[1:], jnp.bfloat16),
+        in_specs=[pl.BlockSpec(memory_space=pltpu.VMEM)] * 2,
+        out_specs=pl.BlockSpec(memory_space=pltpu.VMEM),
+        cost_estimate=pl.CostEstimate(flops=4_000_000, bytes_accessed=409600, transcendentals=0),
+        compiler_params=pltpu.CompilerParams(vmem_limit_bytes=VMEM_BYTES),
+        name="scaled_copies",
+    )(parts, pair)
 
 
 def on_device(grad_out, hidden, error, q_prev):
@@ -127,25 +163,25 @@
     half = q_local.shape[1] // 2
     left, right = q_local[:, :half], q_local[:, half:]
     other = swap(jnp.where(first, right, left).astype(bf16))
-    other_rows = swap(gram_rows)
-    gram_rows = jnp.concatenate(
-        [jnp.where(first, gram_rows, other_rows), jnp.where(first, other_rows, gram_rows)]
-    )
+    gram_rows = jnp.pad(gram_rows, ((0, 8 - some), (0, 0)))
     q_pair = (jnp.where(first, left, right) + other.astype(f32)).astype(bf16)
     gram_rows = jnp.broadcast_to(gram_rows[None], (plane,) + gram_rows.shape)
     got = exchange(jnp.concatenate([by_lanes(q_pair, plane), gram_rows], axis=1), PLANE)
     q_share = total(got[:, :rank]).astype(bf16)
     q_share, got = lax.optimization_barrier((q_share, got))
-    inverse, pair = inverse_factor(got, rank)
-    q_share = total(spread(q_share, "z"))
-    q_share = jnp.dot(inverse / groups, q_share, precision=lax.Precision.HIGHEST).astype(bf16)
-    mine = spread(q_share, PLANE).transpose(1, 0, 2).reshape(rank, -1)
+    own_rows = got[: plane // 2, rank:]
+    other_rows = swap(own_rows)
+    zero_rows = jnp.where(first, own_rows, other_rows)
+    one_rows = jnp.where(first, other_rows, own_rows)
+    q_factors, p_factors = inverse_factor(zero_rows, one_rows, rank)
+    q_copies = scaled_copies(spread(q_share, "z"), q_factors, plane)
+    mine = exchange(q_copies, PLANE).transpose(1, 0, 2).reshape(rank, -1)
     other = swap(mine)
     q_factor = jnp.concatenate(
         [jnp.where(first, mine, other), jnp.where(first, other, mine)], axis=1
     ).T
     twice = jnp.concatenate([p_sum, p_sum], axis=1)
-    p_factor = contract(twice, pair, ((1,), (1,))).astype(bf16)
+    p_factor = contract(twice, p_factors, ((1,), (1,))).astype(bf16)
     return (p_factor, q_factor)
 
 

time: 118 us -> 118 us (level)
  waiting for transfers between devices: 11.2 us -> 14.3 us
  matrix products: 20.8 us -> 19.1 us
  Pallas kernels: 5.34 us -> 3.95 us
    all_to_all x3, waiting for transfers between devices: 9.79 us -> 13 us  [exchange(): return lax.all_to_all(parts, axis, split_axis=0, concat_axis=0, tiled=True)]
    pallas_call x1 -> x2, Pallas kernels: 5.34 us -> 3.95 us  [the longest x1 3.78 us: inverse_factor(): pl.pallas_call(eliminate, out_shape=[pair, pair], in_specs=[pl.BlockSpec(...]
  transfers between devices with their start and end apart: 6 -> 6, of which waited for: 5 -> 5; matrix products, arithmetic and copies ran while one was open for 10% -> 10% of each run, Pallas kernels for 5% -> 3%
where the time goes in v2:
time: 118 us; the launch traced here: 117 us
  blocking collectives  49.4 us (42%)
  starting transfers between devices  23.4 us (20%)
  matrix products  19.1 us (16%)
  waiting for transfers between devices  14.3 us (12%)
  Pallas kernels  3.95 us (3%)
  local copies, waits for them, and re-layouts  3.69 us (3%)
  other arithmetic  2.23 us (2%)
    all_to_all x4, blocking collectives, exchange(): return lax.all_to_all(parts, axis, split_axis=0, concat_axis=0, tiled=True)  49.4 us
    all_to_all x3, starting transfers between devices, exchange(): return lax.all_to_all(parts, axis, split_axis=0, concat_axis=0, tiled=True)  19.2 us
    all_to_all x3, waiting for transfers between devices, exchange(): return lax.all_to_all(parts, axis, split_axis=0, concat_axis=0, tiled=True)  13 us
    dot_general x6, matrix products, contract(): lax.dot_general(left, right, (dims, ((), ())), preferred_element_type=jnp...  12 us
    dot_general x1, matrix products, on_device(): base = jnp.dot(e_rows, q_prev, preferred_element_type=f32)  5.6 us
    ppermute x3, starting transfers between devices, swap(): return lax.ppermute(block, 'core', [(0, 1), (1, 0)])  4.13 us
    pallas_call x1, Pallas kernels, inverse_factor(): pl.pallas_call(eliminate, out_shape=[pair, pair], in_specs=[pl.BlockSpec(...  3.78 us
  transfers between devices with their start and end apart: 6, of which 5 were waited for; matrix products, arithmetic and copies ran while one was open for 10% of the time, Pallas kernels for 3%

profile of v2, /device:TPU:1, one launch (start us, length us, event | category | flops | bytes accessed | tf_op | source)
XLA Modules:
  0.0 116.9 jit_solution(10221791720343779806)
XLA Ops:
  0.6 0.0 copy-start
  0.6 1.2 %copy-done = bf16[1,128,4096]{2,1,0:T(8,128)(2,1)S(1)} copy-done((bf16[1,128,4096]{2,1,0:T(8,128)(2,1)S(1)}, bf16[1,128,4096]{2,1,0:T(8,128)(2,1)}, u32[]{:S(2)}) %copy-start) | copy-done | bytes 1048600
  1.9 1.5 %convolution_convert_fusion.1 = bf16[128,64]{0,1:T(8,128)(2,1)S(1)} fusion(bf16[4096,64]{0,1:T(8,128)(2,1)} %param.7, bf16[1,128,4096]{2,1,0:T(8,128)(2,1)S(1)} %copy-done), kind=kOutput, calls=%fused_computation.16 | convolution fusion | flops 67117056 | bytes 1589248 | tf_op jit(solution)/shard_map/dot_general | solution.py:146
  3.4 0.8 broadcast_in_dim.8
  4.1 8.4 %all-to-all-start = ((bf16[16,128,64]{1,2,0:T(8,128)(2,1)}), bf16[16,128,64]{1,2,0:T(8,128)(2,1)S(1)}, u32[]{:S(2)}, u32[]{:S(2)}) async-start(bf16[16,128,64]{1,2,0:T(8,128)(2,1)} %broadcast_in_dim.8), calls=%async_computation | async-start | bytes 524288 | tf_op jit(solution)/shard_map/all_to_all | solution.py:26
  12.6 5.6 %fusion.2 = f32[896,64]{0,1:T(8,128)S(1)} fusion(bf16[4096,64]{0,1:T(8,128)(2,1)} %param.7, bf16[1,896,4096]{2,1,0:T(8,128)(2,1)} %param.6), kind=kOutput, calls=%fused_computation.2 | convolution fusion | flops 469762048 | bytes 8093696 | tf_op jit(solution)/shard_map/dot_general | solution.py:149
  18.2 3.1 %all-to-all-done = bf16[16,128,64]{1,2,0:T(8,128)(2,1)S(1)} async-done(((bf16[16,128,64]{1,2,0:T(8,128)(2,1)}), bf16[16,128,64]{1,2,0:T(8,128)(2,1)S(1)}, u32[]{:S(2)}, u32[]{:S(2)}) %all-to-all-start) | async-done | bytes 262176 | tf_op jit(solution)/shard_map/all_to_all | solution.py:26
  21.3 2.8 %fusion.20 = bf16[896,64]{0,1:T(8,128)(2,1)S(1)} fusion(f32[896,64]{0,1:T(8,128)S(1)} %fusion.2, bf16[1,2048,896]{2,1,0:T(8,128)(2,1)} %param.5, bf16[16,128,64]{1,2,0:T(8,128)(2,1)S(1)} %all-to-all-done), kind=kOutput, calls=%fused_computation.13 | convolution fusion | flops 234995712 | bytes 4276224 | tf_op jit(solution)/shard_map/dot_general | solution.py:22
  24.0 0.2 copy.25
  24.2 0.2 reshape.37
  24.4 16.6 %all_to_all.35 = bf16[16,2,1792]{2,1,0:T(2,128)(2,1)S(1)} all-to-all(bf16[16,2,1792]{2,1,0:T(2,128)(2,1)S(1)} %reshape.37), channel_id=1, replica_groups=mesh['z'=8,'ylo'=2,'yhi'=2,'x'=4,'core'=2] {'z','ylo'}, dimensions={0} | all-to-all | bytes 229376 | tf_op jit(solution)/shard_map/all_to_all | solution.py:26
  41.0 0.2 reshape.38
  41.2 0.1 reduce_sum.45
  41.3 0.2 reshape.39
  41.5 11.0 %all_to_all.36 = bf16[16,2,1792]{2,1,0:T(2,128)(2,1)S(1)} all-to-all(bf16[16,2,1792]{2,1,0:T(2,128)(2,1)S(1)} %reshape.39), channel_id=1, replica_groups=mesh['z'=8,'ylo'=2,'yhi'=2,'x'=4,'core'=2] {'z','ylo'}, dimensions={0} | all-to-all | bytes 229376 | tf_op jit(solution)/shard_map/all_to_all | solution.py:26
  52.5 0.2 reshape.40
  52.7 0.2 reduce-precision_convert_fusion
  52.9 3.3 %fusion.11 = bf16[8,16,8,128]{3,2,1,0:T(8,128)(2,1)S(1)} fusion(bf16[896,64]{1,0:T(8,128)(2,1)S(1)} %bitcast.80, bf16[1,2048,896]{2,1,0:T(8,128)(2,1)} %param.5), kind=kOutput, calls=%fused_computation.10 | convolution fusion | flops 235012096 | bytes 4046848 | tf_op jit(solution)/shard_map/dot_general | solution.py:22
  56.2 0.1 copy.42
  56.3 0.1 pad_maximum_fusion.1
  56.3 0.7 fusion.26
  57.1 7.4 %all-to-all-start.3 = ((bf16[16,72,128]{2,1,0:T(8,128)(2,1)}), bf16[16,72,128]{2,1,0:T(8,128)(2,1)S(1)}, u32[]{:S(2)}, u32[]{:S(2)}) async-start(bf16[16,72,128]{2,1,0:T(8,128)(2,1)} %fusion.26), calls=%async_computation.3 | async-start | bytes 589824 | tf_op jit(solution)/shard_map/all_to_all | solution.py:26
  64.5 4.5 %fusion = f32[64,4096]{1,0:T(8,128)S(1)} fusion(bf16[896,64]{1,0:T(8,128)(2,1)S(1)} %bitcast.81, bf16[1,896,4096]{2,1,0:T(8,128)(2,1)} %param.6), kind=kOutput, calls=%fused_computation | convolution fusion | flops 469762048 | bytes 8503296 | tf_op jit(solution)/shard_map/dot_general | solution.py:22
  69.0 4.4 %all-to-all-done.3 = bf16[16,72,128]{2,1,0:T(8,128)(2,1)S(1)} async-done(((bf16[16,72,128]{2,1,0:T(8,128)(2,1)}), bf16[16,72,128]{2,1,0:T(8,128)(2,1)S(1)}, u32[]{:S(2)}, u32[]{:S(2)}) %all-to-all-start.3) | async-done | bytes 294944 | tf_op jit(solution)/shard_map/all_to_all | solution.py:26
  73.4 0.3 convolution_add_fusion
  73.7 0.1 select_convert_fusion
  73.8 1.0 collective-permute-start
  74.8 0.1 reduce-precision_convert_fusion.1
  74.9 0.1 fusion.37
  75.0 1.0 collective-permute-done
  75.9 0.1 bitcast_bitcast_fusion
  76.1 11.1 %all_to_all.37 = bf16[16,72,128]{2,1,0:T(8,128)(2,1)S(1)} all-to-all(bf16[16,72,128]{2,1,0:T(8,128)(2,1)S(1)} %pad_maximum_fusion), channel_id=1, replica_groups=mesh['z'=8,'ylo'=2,'yhi'=2,'x'=4,'core'=2] {'ylo','yhi','x'}, dimensions={0} | all-to-all | bytes 589824 | tf_op jit(solution)/shard_map/all_to_all | solution.py:26
  87.2 1.6 %collective-permute-start.1 = (bf16[8,8,128]{2,1,0:T(8,128)(2,1)S(1)}, bf16[8,8,128]{2,1,0:T(8,128)(2,1)S(1)}, u32[]{:S(2)}, u32[]{:S(2)}) collective-permute-start(bf16[8,8,128]{2,1,0:T(8,128)(2,1)S(1)} %slice.31), channel_id=1, source_target_pairs={{0,1},{1,0},{2,3},{3,2},{4,5},{5,4},{6,7},{7,6},{8,9},{9,8},{10,11... | collective-permute-start | bytes 49160 | tf_op jit(solution)/shard_map/ppermute | solution.py:35
  88.8 0.7 broadcast_in_dim.11
  89.5 3.4 %all-to-all-start.5 = ((bf16[8,64,128]{2,1,0:T(8,128)(2,1)}), bf16[8,64,128]{2,1,0:T(8,128)(2,1)S(1)}, u32[]{:S(2)}, u32[]{:S(2)}) async-start(bf16[8,64,128]{2,1,0:T(8,128)(2,1)} %broadcast_in_dim.11), calls=%async_computation.5 | async-start | bytes 262144 | tf_op jit(solution)/shard_map/all_to_all | solution.py:26
  92.9 0.0 collective-permute-done.1
  92.9 3.8 %inverse_factor.1 = (bf16[64,128]{1,0:T(8,128)(2,1)S(1)}, bf16[64,128]{1,0:T(8,128)(2,1)S(1)}) custom-call(bf16[8,8,128]{2,1,0:T(8,128)(2,1)S(1)} %get-tuple-element.17.zero_ref, bf16[8,8,128]{2,1,0:T(8,128)(2,1)S(1)} %get-tuple-element.16.one_ref), custom_call_target="tpu_custom_call" | custom-call | flops 4000000000 | bytes 49152 | tf_op jit(solution)/shard_map/inverse_factor/pallas_call | solution.py:99
  96.7 5.6 %all-to-all-done.5.parts_ref = bf16[8,64,128]{2,1,0:T(8,128)(2,1)S(1)} async-done(((bf16[8,64,128]{2,1,0:T(8,128)(2,1)}), bf16[8,64,128]{2,1,0:T(8,128)(2,1)S(1)}, u32[]{:S(2)}, u32[]{:S(2)}) %all-to-all-start.5) | async-done | bytes 131104 | tf_op jit(solution)/shard_map/all_to_all | solution.py:26
  102.2 0.2 scaled_copies.1
  102.4 10.8 %all_to_all.38 = bf16[16,64,128]{2,1,0:T(8,128)(2,1)S(1)} all-to-all(bf16[16,64,128]{2,1,0:T(8,128)(2,1)S(1)} %scaled_copies.1), channel_id=1, replica_groups=mesh['z'=8,'ylo'=2,'yhi'=2,'x'=4,'core'=2] {'ylo','yhi','x'}, dimensions={0} | all-to-all | bytes 524288 | tf_op jit(solution)/shard_map/all_to_all | solution.py:26
  113.2 1.6 %collective-permute-start.2 = (bf16[64,2048]{1,0:T(8,128)(2,1)S(1)}, bf16[64,2048]{1,0:T(8,128)(2,1)S(1)}, u32[]{:S(2)}, u32[]{:S(2)}) collective-permute-start(bf16[64,2048]{1,0:T(8,128)(2,1)S(1)} %copy_bitcast_fusion), channel_id=1, source_target_pairs={{0,1},{1,0},{2,3},{3,2},{4,5},{5,4},{6,7},{7,6},{8,9},{9,8},{10,11... | collective-permute-start | bytes 786440 | tf_op jit(solution)/shard_map/ppermute | solution.py:35
  114.8 0.9 convolution_convert_fusion
  115.7 0.2 collective-permute-done.2
  115.9 0.1 broadcast_select_fusion.1
  116.0 0.8 maximum_bitcast_fusion
  (9 shorter events, 0.2 us)
Async XLA Ops:
  0.6 1.2 %copy-start = (bf16[1,128,4096]{2,1,0:T(8,128)(2,1)S(1)}, bf16[1,128,4096]{2,1,0:T(8,128)(2,1)}, u32[]{:S(2)}) copy-start(bf16[1,128,4096]{2,1,0:T(8,128)(2,1)} %param.4) | copy-start | bytes 3145732
  4.1 17.1 %all-to-all-start = ((bf16[16,128,64]{1,2,0:T(8,128)(2,1)}), bf16[16,128,64]{1,2,0:T(8,128)(2,1)S(1)}, u32[]{:S(2)}, u32[]{:S(2)}) async-start(bf16[16,128,64]{1,2,0:T(8,128)(2,1)} %broadcast_in_dim.8), calls=%async_computation | async-start | bytes 524288 | tf_op jit(solution)/shard_map/all_to_all | solution.py:26
  57.1 16.3 %all-to-all-start.3 = ((bf16[16,72,128]{2,1,0:T(8,128)(2,1)}), bf16[16,72,128]{2,1,0:T(8,128)(2,1)S(1)}, u32[]{:S(2)}, u32[]{:S(2)}) async-start(bf16[16,72,128]{2,1,0:T(8,128)(2,1)} %fusion.26), calls=%async_computation.3 | async-start | bytes 589824 | tf_op jit(solution)/shard_map/all_to_all | solution.py:26
  73.8 2.2 %collective-permute-start = (bf16[64,2048]{1,0:T(8,128)(2,1)S(1)}, bf16[64,2048]{1,0:T(8,128)(2,1)S(1)}, u32[]{:S(2)}, u32[]{:S(2)}) collective-permute-start(bf16[64,2048]{1,0:T(8,128)(2,1)S(1)} %select_convert_fusion), channel_id=1, source_target_pairs={{0,1},{1,0},{2,3},{3,2},{4,5},{5,4},{6,7},{7,6},{8,9},{9,8},{10,11... | collective-permute-start | bytes 786440 | tf_op jit(solution)/shard_map/ppermute | solution.py:35
  87.2 5.6 %collective-permute-start.1 = (bf16[8,8,128]{2,1,0:T(8,128)(2,1)S(1)}, bf16[8,8,128]{2,1,0:T(8,128)(2,1)S(1)}, u32[]{:S(2)}, u32[]{:S(2)}) collective-permute-start(bf16[8,8,128]{2,1,0:T(8,128)(2,1)S(1)} %slice.31), channel_id=1, source_target_pairs={{0,1},{1,0},{2,3},{3,2},{4,5},{5,4},{6,7},{7,6},{8,9},{9,8},{10,11... | collective-permute-start | bytes 49160 | tf_op jit(solution)/shard_map/ppermute | solution.py:35
  89.5 12.8 %all-to-all-start.5 = ((bf16[8,64,128]{2,1,0:T(8,128)(2,1)}), bf16[8,64,128]{2,1,0:T(8,128)(2,1)S(1)}, u32[]{:S(2)}, u32[]{:S(2)}) async-start(bf16[8,64,128]{2,1,0:T(8,128)(2,1)} %broadcast_in_dim.11), calls=%async_computation.5 | async-start | bytes 262144 | tf_op jit(solution)/shard_map/all_to_all | solution.py:26
  113.2 2.7 %collective-permute-start.2 = (bf16[64,2048]{1,0:T(8,128)(2,1)S(1)}, bf16[64,2048]{1,0:T(8,128)(2,1)S(1)}, u32[]{:S(2)}, u32[]{:S(2)}) collective-permute-start(bf16[64,2048]{1,0:T(8,128)(2,1)S(1)} %copy_bitcast_fusion), channel_id=1, source_target_pairs={{0,1},{1,0},{2,3},{3,2},{4,5},{5,4},{6,7},{7,6},{8,9},{9,8},{10,11... | collective-permute-start | bytes 786440 | tf_op jit(solution)/shard_map/ppermute | solution.py:35

commit v3 on v2

--- a/solution.py
+++ b/solution.py
@@ -11,6 +11,7 @@
 FF = 14336
 GROUPS = 16
 VMEM_BYTES = 4 << 20
+ROWS, LANES = 32, 128
 AXES = ("z", "ylo", "yhi", "x", "core")
 SIZES = (-1, 2, 2, 4, 2)
 DP = ("z", "ylo")
@@ -51,6 +52,65 @@
 
 def by_lanes(array, count):
     return array.reshape(array.shape[0], count, -1).transpose(1, 0, 2)
+
+
+def places(units):
+    return [(r, c) for r in (0, ROWS) for c in range(0, units, LANES)]
+
+
+def left_kernel(proj_ref, h_ref, base_ref, out_ref):
+    proj = jnp.concatenate([proj_ref[j] for j in range(proj_ref.shape[0])], axis=1)
+    terms = base_ref[...] + contract(proj, h_ref[...], ((1,), (0,)))
+    terms = terms.astype(jnp.bfloat16)
+    used = places(terms.shape[1])
+    for j, (r, c) in enumerate(used):
+        out_ref[j] = terms[r : r + ROWS, c : c + LANES]
+    for j in range(len(used), out_ref.shape[0]):
+        out_ref[j] = jnp.zeros((ROWS, LANES), jnp.bfloat16)
+
+
+def left_terms(proj, h_rows, base, count):
+    return pl.pallas_call(
+        left_kernel,
+        out_shape=jax.ShapeDtypeStruct((count, ROWS, LANES), jnp.bfloat16),
+        in_specs=[pl.BlockSpec(memory_space=pltpu.VMEM)] * 3,
+        out_specs=pl.BlockSpec(memory_space=pltpu.VMEM),
+        cost_estimate=pl.CostEstimate(flops=1_000_000_000, bytes_accessed=4 << 20, transcendentals=0),
+        compiler_params=pltpu.CompilerParams(vmem_limit_bytes=3 * VMEM_BYTES),
+        name="left_terms",
+    )(proj, h_rows, base)
+
+
+def mix_kernel(parts_ref, h_ref, out_ref, p_ref):
+    for j, (r, c) in enumerate(places(p_ref.shape[1])):
+        p_ref[r : r + ROWS, c : c + LANES] = parts_ref[j]
+    p = p_ref[...]
+    gram = contract(p, p, ((1,), (1,)))
+    high = gram.astype(jnp.bfloat16).astype(jnp.float32)
+    pair = jnp.concatenate([high, gram - high], axis=1)
+    mixed = contract(p, h_ref[...], ((1,), (1,))).astype(jnp.bfloat16)
+    count = out_ref.shape[0]
+    some = pair.shape[0] // count
+    fill = jnp.zeros((8 - some, LANES), jnp.float32)
+    for j in range(count):
+        rows = jnp.concatenate([pair[some * j : some * (j + 1)], fill], axis=0)
+        block = mixed[:, j * LANES : (j + 1) * LANES]
+        out_ref[j] = jnp.concatenate([block, rows.astype(jnp.bfloat16)], axis=0)
+
+
+def mixed_terms(parts, h_rows, rank, units, count):
+    return pl.pallas_call(
+        mix_kernel,
+        out_shape=[
+            jax.ShapeDtypeStruct((count, rank + 8, LANES), jnp.bfloat16),
+            jax.ShapeDtypeStruct((rank, units), jnp.bfloat16),
+        ],
+        in_specs=[pl.BlockSpec(memory_space=pltpu.VMEM)] * 2,
+        out_specs=[pl.BlockSpec(memory_space=pltpu.VMEM)] * 2,
+        cost_estimate=pl.CostEstimate(flops=1_000_000_000, bytes_accessed=4 << 20, transcendentals=0),
+        compiler_params=pltpu.CompilerParams(vmem_limit_bytes=3 * VMEM_BYTES),
+        name="mixed_terms",
+    )(parts, h_rows)
 
 
 def eliminate(zero_ref, one_ref, q_pair_ref, p_pair_ref, inverse_ref):
@@ -145,21 +205,16 @@
 
     proj_local = jnp.dot(g_rows, q_prev, preferred_element_type=f32).astype(bf16)
     first, proj_local = lax.optimization_barrier((lax.axis_index("core") == 0, proj_local))
-    proj = spread(proj_local, MP).reshape(h_rows.shape[0], rank)
-    base = jnp.dot(e_rows, q_prev, preferred_element_type=f32)
-    p_local = base + contract(h_rows, proj, ((0,), (0,)))
-    p_terms = p_local.astype(bf16).reshape(groups, units // groups, rank)
+    proj = spread(proj_local.T, MP)
+    base = jnp.dot(e_rows, q_prev, preferred_element_type=f32).T
+    p_terms = left_terms(proj, h_rows, base, groups)
     p_part = total(exchange(p_terms, DP)).astype(bf16)
-    p_sum = spread(p_part, DP).reshape(units, rank)
-
-    gram_terms = jnp.concatenate(halves(contract(p_sum, p_sum, ((0,), (0,)))), axis=1)
-    gram_terms = jnp.pad(gram_terms.reshape(parts, some, -1), ((0, 0), (0, 8 - some), (0, 0)))
-    mixed_terms = by_lanes(contract(p_sum, h_rows, ((0,), (1,))).astype(bf16), parts)
-    got = exchange(jnp.concatenate([mixed_terms, gram_terms], axis=1), MP)
+    parts_of_mixed, p_sum = mixed_terms(spread(p_part, DP), h_rows, rank, units, parts)
+    got = exchange(parts_of_mixed, MP)
     mixed = total(got[:, :rank]).astype(bf16)
     gram_rows = jnp.concatenate(halves(whole(total(got[:, rank : rank + some]))), axis=1)
 
-    q_local = contract(p_sum, e_rows, ((0,), (0,))) + contract(mixed, g_rows, ((1,), (0,)))
+    q_local = contract(p_sum, e_rows, ((1,), (0,))) + contract(mixed, g_rows, ((1,), (0,)))
     half = q_local.shape[1] // 2
     left, right = q_local[:, :half], q_local[:, half:]
     other = swap(jnp.where(first, right, left).astype(bf16))
@@ -180,8 +235,8 @@
     q_factor = jnp.concatenate(
         [jnp.where(first, mine, other), jnp.where(first, other, mine)], axis=1
     ).T
-    twice = jnp.concatenate([p_sum, p_sum], axis=1)
-    p_factor = contract(twice, p_factors, ((1,), (1,))).astype(bf16)
+    twice = jnp.concatenate([p_sum, p_sum], axis=0)
+    p_factor = contract(p_factors, twice, ((1,), (0,))).astype(bf16).T
     return (p_factor, q_factor)
 
 

time: 118 us -> 117 us (level)
  matrix products: 19.1 us -> 12.7 us
  local copies, waits for them, and re-layouts: 3.69 us -> 6.78 us
  Pallas kernels: 3.95 us -> 6.69 us
    dot_general x6 -> x3, matrix products: 12 us -> 5.62 us  [contract(): lax.dot_general(left, right, (dims, ((), ())), preferred_element_type=jnp...]
    unnamed x6, local copies, waits for them, and re-layouts: 1.95 us -> 5.29 us
    pallas_call x0 -> x2, Pallas kernels: none -> 2.74 us  [the longest x1 2.01 us: mixed_terms(): pl.pallas_call(mix_kernel, out_shape=[jax.ShapeDtypeStruct((count, rank +...]
where the time goes in v3:
time: 117 us; the launch traced here: 116 us
  blocking collectives  49.7 us (42%)
  starting transfers between devices  23.7 us (20%)
  waiting for transfers between devices  14.3 us (12%)
  matrix products  12.7 us (11%)
  local copies, waits for them, and re-layouts  6.78 us (6%)
  Pallas kernels  6.69 us (6%)
  other arithmetic  1.38 us (1%)
    all_to_all x4, blocking collectives, exchange(): return lax.all_to_all(parts, axis, split_axis=0, concat_axis=0, tiled=True)  49.7 us
    all_to_all x3, starting transfers between devices, exchange(): return lax.all_to_all(parts, axis, split_axis=0, concat_axis=0, tiled=True)  19.5 us
    all_to_all x3, waiting for transfers between devices, exchange(): return lax.all_to_all(parts, axis, split_axis=0, concat_axis=0, tiled=True)  13 us
    dot_general x3, matrix products, contract(): lax.dot_general(left, right, (dims, ((), ())), preferred_element_type=jnp...  5.62 us
    dot_general x1, matrix products, on_device(): base = jnp.dot(e_rows, q_prev, preferred_element_type=f32).T  5.61 us
    unnamed x6, local copies, waits for them, and re-layouts  5.29 us
    ppermute x3, starting transfers between devices, swap(): return lax.ppermute(block, 'core', [(0, 1), (1, 0)])  4.13 us
    pallas_call x1, Pallas kernels, inverse_factor(): pl.pallas_call(eliminate, out_shape=[pair, pair], in_specs=[pl.BlockSpec(...  3.78 us
  transfers between devices with their start and end apart: 6, of which 5 were waited for; matrix products, arithmetic and copies ran while one was open for 10% of the time, Pallas kernels for 3%

profile of v3, /device:TPU:1, one launch (start us, length us, event | category | flops | bytes accessed | tf_op | source)
XLA Modules:
  0.0 116.1 jit_solution(14979206220901013337)
XLA Ops:
  0.6 0.0 copy-start
  0.6 1.2 %copy-done = bf16[1,128,4096]{2,1,0:T(8,128)(2,1)S(1)} copy-done((bf16[1,128,4096]{2,1,0:T(8,128)(2,1)S(1)}, bf16[1,128,4096]{2,1,0:T(8,128)(2,1)}, u32[]{:S(2)}) %copy-start) | copy-done | bytes 1048600
  1.9 1.5 %convolution_convert_fusion.1 = bf16[128,64]{0,1:T(8,128)(2,1)S(1)} fusion(bf16[4096,64]{0,1:T(8,128)(2,1)} %param.7, bf16[1,128,4096]{2,1,0:T(8,128)(2,1)S(1)} %copy-done), kind=kOutput, calls=%fused_computation.6 | convolution fusion | flops 67117056 | bytes 1589248 | tf_op jit(solution)/shard_map/dot_general | solution.py:206
  3.4 0.8 broadcast_in_dim.8
  4.1 8.4 %all-to-all-start = ((bf16[16,64,128]{2,1,0:T(8,128)(2,1)}), bf16[16,64,128]{2,1,0:T(8,128)(2,1)S(1)}, u32[]{:S(2)}, u32[]{:S(2)}) async-start(bf16[16,64,128]{2,1,0:T(8,128)(2,1)} %broadcast_in_dim.8), calls=%async_computation | async-start | bytes 524288 | tf_op jit(solution)/shard_map/all_to_all | solution.py:27
  12.6 5.6 %fusion.2.base_ref = f32[64,896]{1,0:T(8,128)S(1)} fusion(bf16[4096,64]{0,1:T(8,128)(2,1)} %param.7, bf16[1,896,4096]{2,1,0:T(8,128)(2,1)} %param.6), kind=kOutput, calls=%fused_computation.2 | convolution fusion | flops 469762048 | bytes 8093696 | tf_op jit(solution)/shard_map/dot_general | solution.py:209
  18.2 3.1 %all-to-all-done.proj_ref = bf16[16,64,128]{2,1,0:T(8,128)(2,1)S(1)} async-done(((bf16[16,64,128]{2,1,0:T(8,128)(2,1)}), bf16[16,64,128]{2,1,0:T(8,128)(2,1)S(1)}, u32[]{:S(2)}, u32[]{:S(2)}) %all-to-all-start) | async-done | bytes 262176 | tf_op jit(solution)/shard_map/all_to_all | solution.py:27
  21.3 0.0 copy-start.1
  21.3 2.0 %copy-done.1 = bf16[1,2048,896]{2,1,0:T(8,128)(2,1)S(1)} copy-done((bf16[1,2048,896]{2,1,0:T(8,128)(2,1)S(1)}, bf16[1,2048,896]{2,1,0:T(8,128)(2,1)}, u32[]{:S(2)}) %copy-start.1) | copy-done | bytes 3670040
  23.3 0.7 left_terms.1
  24.0 16.7 %all_to_all.35 = bf16[16,32,128]{2,1,0:T(8,128)(2,1)S(1)} all-to-all(bf16[16,32,128]{2,1,0:T(8,128)(2,1)S(1)} %left_terms.1), channel_id=1, replica_groups=mesh['z'=8,'ylo'=2,'yhi'=2,'x'=4,'core'=2] {'z','ylo'}, dimensions={0} | all-to-all | bytes 262144 | tf_op jit(solution)/shard_map/all_to_all | solution.py:27
  40.8 11.1 %all_to_all.36.parts_ref = bf16[16,32,128]{2,1,0:T(8,128)(2,1)S(1)} all-to-all(bf16[16,32,128]{2,1,0:T(8,128)(2,1)S(1)} %broadcast_in_dim.9), channel_id=1, replica_groups=mesh['z'=8,'ylo'=2,'yhi'=2,'x'=4,'core'=2] {'z','ylo'}, dimensions={0} | all-to-all | bytes 262144 | tf_op jit(solution)/shard_map/all_to_all | solution.py:27
  51.9 0.0 copy-start.2
  51.9 2.0 %copy-done.2 = bf16[1,2048,896]{2,1,0:T(8,128)(2,1)S(1)} copy-done((bf16[1,2048,896]{2,1,0:T(8,128)(2,1)S(1)}, bf16[1,2048,896]{2,1,0:T(8,128)(2,1)}, u32[]{:S(2)}) %copy-start.2) | copy-done | bytes 3670040
  54.0 2.0 %mixed_terms.1 = (bf16[16,72,128]{2,1,0:T(8,128)(2,1)}, bf16[64,896]{1,0:T(8,128)(2,1)S(1)}) custom-call(bf16[16,32,128]{2,1,0:T(8,128)(2,1)S(1)} %all_to_all.36.parts_ref, bf16[2048,896]{1,0:T(8,128)(2,1)S(1)} %bitcast.39), custom_call_target="tpu_custom_call" | custom-call | flops 1000000000 | bytes 4194304 | tf_op jit(solution)/shard_map/mixed_terms/pallas_call | solution.py:102
  56.0 7.7 %all-to-all-start.3 = ((bf16[16,72,128]{2,1,0:T(8,128)(2,1)}), bf16[16,72,128]{2,1,0:T(8,128)(2,1)S(1)}, u32[]{:S(2)}, u32[]{:S(2)}) async-start(bf16[16,72,128]{2,1,0:T(8,128)(2,1)} %get-tuple-element.13), calls=%async_computation.3 | async-start | bytes 589824 | tf_op jit(solution)/shard_map/all_to_all | solution.py:27
  63.7 4.5 %fusion = f32[64,4096]{1,0:T(8,128)S(1)} fusion(bf16[64,896]{1,0:T(8,128)(2,1)S(1)} %get-tuple-element.11, bf16[1,896,4096]{2,1,0:T(8,128)(2,1)} %param.6), kind=kOutput, calls=%fused_computation | convolution fusion | flops 469762048 | bytes 8503296 | tf_op jit(solution)/shard_map/dot_general | solution.py:23
  68.2 4.4 %all-to-all-done.3 = bf16[16,72,128]{2,1,0:T(8,128)(2,1)S(1)} async-done(((bf16[16,72,128]{2,1,0:T(8,128)(2,1)}), bf16[16,72,128]{2,1,0:T(8,128)(2,1)S(1)}, u32[]{:S(2)}, u32[]{:S(2)}) %all-to-all-start.3) | async-done | bytes 294944 | tf_op jit(solution)/shard_map/all_to_all | solution.py:27
  72.6 0.3 convolution_add_fusion
  72.9 0.1 select_convert_fusion
  73.0 1.0 collective-permute-start
  74.0 0.1 reduce-precision_convert_fusion
  74.1 0.1 fusion.13
  74.2 1.0 collective-permute-done
  75.2 0.1 bitcast_bitcast_fusion
  75.3 11.1 %all_to_all.37 = bf16[16,72,128]{2,1,0:T(8,128)(2,1)S(1)} all-to-all(bf16[16,72,128]{2,1,0:T(8,128)(2,1)S(1)} %pad_maximum_fusion), channel_id=1, replica_groups=mesh['z'=8,'ylo'=2,'yhi'=2,'x'=4,'core'=2] {'ylo','yhi','x'}, dimensions={0} | all-to-all | bytes 589824 | tf_op jit(solution)/shard_map/all_to_all | solution.py:27
  86.4 1.6 %collective-permute-start.1 = (bf16[8,8,128]{2,1,0:T(8,128)(2,1)S(1)}, bf16[8,8,128]{2,1,0:T(8,128)(2,1)S(1)}, u32[]{:S(2)}, u32[]{:S(2)}) collective-permute-start(bf16[8,8,128]{2,1,0:T(8,128)(2,1)S(1)} %slice.31), channel_id=1, source_target_pairs={{0,1},{1,0},{2,3},{3,2},{4,5},{5,4},{6,7},{7,6},{8,9},{9,8},{10,11... | collective-permute-start | bytes 49160 | tf_op jit(solution)/shard_map/ppermute | solution.py:36
  88.0 0.7 broadcast_in_dim.11
  88.7 3.4 %all-to-all-start.5 = ((bf16[8,64,128]{2,1,0:T(8,128)(2,1)}), bf16[8,64,128]{2,1,0:T(8,128)(2,1)S(1)}, u32[]{:S(2)}, u32[]{:S(2)}) async-start(bf16[8,64,128]{2,1,0:T(8,128)(2,1)} %broadcast_in_dim.11), calls=%async_computation.5 | async-start | bytes 262144 | tf_op jit(solution)/shard_map/all_to_all | solution.py:27
  92.1 0.0 collective-permute-done.1
  92.1 3.8 %inverse_factor.1 = (bf16[64,128]{1,0:T(8,128)(2,1)S(1)}, bf16[64,128]{1,0:T(8,128)(2,1)S(1)}) custom-call(bf16[8,8,128]{2,1,0:T(8,128)(2,1)S(1)} %get-tuple-element.21.zero_ref, bf16[8,8,128]{2,1,0:T(8,128)(2,1)S(1)} %get-tuple-element.20.one_ref), custom_call_target="tpu_custom_call" | custom-call | flops 4000000000 | bytes 49152 | tf_op jit(solution)/shard_map/inverse_factor/pallas_call | solution.py:159
  95.9 5.6 %all-to-all-done.5.parts_ref = bf16[8,64,128]{2,1,0:T(8,128)(2,1)S(1)} async-done(((bf16[8,64,128]{2,1,0:T(8,128)(2,1)}), bf16[8,64,128]{2,1,0:T(8,128)(2,1)S(1)}, u32[]{:S(2)}, u32[]{:S(2)}) %all-to-all-start.5) | async-done | bytes 131104 | tf_op jit(solution)/shard_map/all_to_all | solution.py:27
  101.5 0.2 scaled_copies.1
  101.6 10.8 %all_to_all.38 = bf16[16,64,128]{2,1,0:T(8,128)(2,1)S(1)} all-to-all(bf16[16,64,128]{2,1,0:T(8,128)(2,1)S(1)} %scaled_copies.1), channel_id=1, replica_groups=mesh['z'=8,'ylo'=2,'yhi'=2,'x'=4,'core'=2] {'ylo','yhi','x'}, dimensions={0} | all-to-all | bytes 524288 | tf_op jit(solution)/shard_map/all_to_all | solution.py:27
  112.4 1.6 %collective-permute-start.2 = (bf16[64,2048]{1,0:T(8,128)(2,1)S(1)}, bf16[64,2048]{1,0:T(8,128)(2,1)S(1)}, u32[]{:S(2)}, u32[]{:S(2)}) collective-permute-start(bf16[64,2048]{1,0:T(8,128)(2,1)S(1)} %copy_bitcast_fusion), channel_id=1, source_target_pairs={{0,1},{1,0},{2,3},{3,2},{4,5},{5,4},{6,7},{7,6},{8,9},{9,8},{10,11... | collective-permute-start | bytes 786440 | tf_op jit(solution)/shard_map/ppermute | solution.py:36
  114.0 0.8 convolution_convert_fusion
  114.8 0.3 collective-permute-done.2
  115.1 0.1 broadcast_select_fusion.1
  115.2 0.8 maximum_bitcast_fusion
  (10 shorter events, 0.2 us)
Async XLA Ops:
  0.6 1.2 %copy-start = (bf16[1,128,4096]{2,1,0:T(8,128)(2,1)S(1)}, bf16[1,128,4096]{2,1,0:T(8,128)(2,1)}, u32[]{:S(2)}) copy-start(bf16[1,128,4096]{2,1,0:T(8,128)(2,1)} %param.4) | copy-start | bytes 3145732
  4.1 17.1 %all-to-all-start = ((bf16[16,64,128]{2,1,0:T(8,128)(2,1)}), bf16[16,64,128]{2,1,0:T(8,128)(2,1)S(1)}, u32[]{:S(2)}, u32[]{:S(2)}) async-start(bf16[16,64,128]{2,1,0:T(8,128)(2,1)} %broadcast_in_dim.8), calls=%async_computation | async-start | bytes 524288 | tf_op jit(solution)/shard_map/all_to_all | solution.py:27
  21.3 2.0 %copy-start.1 = (bf16[1,2048,896]{2,1,0:T(8,128)(2,1)S(1)}, bf16[1,2048,896]{2,1,0:T(8,128)(2,1)}, u32[]{:S(2)}) copy-start(bf16[1,2048,896]{2,1,0:T(8,128)(2,1)} %param.5) | copy-start | bytes 11010052
  51.9 2.0 %copy-start.2 = (bf16[1,2048,896]{2,1,0:T(8,128)(2,1)S(1)}, bf16[1,2048,896]{2,1,0:T(8,128)(2,1)}, u32[]{:S(2)}) copy-start(bf16[1,2048,896]{2,1,0:T(8,128)(2,1)} %param.5) | copy-start | bytes 11010052
  56.0 16.6 %all-to-all-start.3 = ((bf16[16,72,128]{2,1,0:T(8,128)(2,1)}), bf16[16,72,128]{2,1,0:T(8,128)(2,1)S(1)}, u32[]{:S(2)}, u32[]{:S(2)}) async-start(bf16[16,72,128]{2,1,0:T(8,128)(2,1)} %get-tuple-element.13), calls=%async_computation.3 | async-start | bytes 589824 | tf_op jit(solution)/shard_map/all_to_all | solution.py:27
  73.0 2.2 %collective-permute-start = (bf16[64,2048]{1,0:T(8,128)(2,1)S(1)}, bf16[64,2048]{1,0:T(8,128)(2,1)S(1)}, u32[]{:S(2)}, u32[]{:S(2)}) collective-permute-start(bf16[64,2048]{1,0:T(8,128)(2,1)S(1)} %select_convert_fusion), channel_id=1, source_target_pairs={{0,1},{1,0},{2,3},{3,2},{4,5},{5,4},{6,7},{7,6},{8,9},{9,8},{10,11... | collective-permute-start | bytes 786440 | tf_op jit(solution)/shard_map/ppermute | solution.py:36
  86.4 5.6 %collective-permute-start.1 = (bf16[8,8,128]{2,1,0:T(8,128)(2,1)S(1)}, bf16[8,8,128]{2,1,0:T(8,128)(2,1)S(1)}, u32[]{:S(2)}, u32[]{:S(2)}) collective-permute-start(bf16[8,8,128]{2,1,0:T(8,128)(2,1)S(1)} %slice.31), channel_id=1, source_target_pairs={{0,1},{1,0},{2,3},{3,2},{4,5},{5,4},{6,7},{7,6},{8,9},{9,8},{10,11... | collective-permute-start | bytes 49160 | tf_op jit(solution)/shard_map/ppermute | solution.py:36
  88.7 12.8 %all-to-all-start.5 = ((bf16[8,64,128]{2,1,0:T(8,128)(2,1)}), bf16[8,64,128]{2,1,0:T(8,128)(2,1)S(1)}, u32[]{:S(2)}, u32[]{:S(2)}) async-start(bf16[8,64,128]{2,1,0:T(8,128)(2,1)} %broadcast_in_dim.11), calls=%async_computation.5 | async-start | bytes 262144 | tf_op jit(solution)/shard_map/all_to_all | solution.py:27
  112.4 2.7 %collective-permute-start.2 = (bf16[64,2048]{1,0:T(8,128)(2,1)S(1)}, bf16[64,2048]{1,0:T(8,128)(2,1)S(1)}, u32[]{:S(2)}, u32[]{:S(2)}) collective-permute-start(bf16[64,2048]{1,0:T(8,128)(2,1)S(1)} %copy_bitcast_fusion), channel_id=1, source_target_pairs={{0,1},{1,0},{2,3},{3,2},{4,5},{5,4},{6,7},{7,6},{8,9},{9,8},{10,11... | collective-permute-start | bytes 786440 | tf_op jit(solution)/shard_map/ppermute | solution.py:36

commit v4 on v3

--- a/solution.py
+++ b/solution.py
@@ -52,6 +52,54 @@
 
 def by_lanes(array, count):
     return array.reshape(array.shape[0], count, -1).transpose(1, 0, 2)
+
+
+def small_call(kernel, outs, *operands, spaces=None, scratch=(), name):
+    spaces = spaces or [pltpu.VMEM] * len(operands)
+    return pl.pallas_call(
+        kernel,
+        out_shape=[jax.ShapeDtypeStruct(shape, dtype) for shape, dtype in outs],
+        in_specs=[pl.BlockSpec(memory_space=space) for space in spaces],
+        out_specs=[pl.BlockSpec(memory_space=pltpu.VMEM)] * len(outs),
+        scratch_shapes=scratch,
+        cost_estimate=pl.CostEstimate(flops=1_000_000_000, bytes_accessed=4 << 20, transcendentals=0),
+        compiler_params=pltpu.CompilerParams(vmem_limit_bytes=3 * VMEM_BYTES),
+        name=name,
+    )(*operands)
+
+
+def project_kernel(q_ref, g_ref, out_ref):
+    proj = contract(q_ref[...], g_ref[...], ((1,), (1,))).astype(jnp.bfloat16)
+    for j in range(out_ref.shape[0]):
+        out_ref[j] = proj
+
+
+def base_kernel(q_ref, e_ref, out_ref, held_ref, arrived):
+    slots = held_ref.shape[0]
+    count = e_ref.shape[0] // LANES
+
+    def fetch(j):
+        rows = e_ref.at[pl.ds(j * LANES, LANES)]
+        return pltpu.make_async_copy(rows, held_ref.at[j % slots], arrived.at[j % slots])
+
+    for j in range(slots - 1):
+        fetch(j).start()
+    for j in range(count):
+        if j + slots - 1 < count:
+            fetch(j + slots - 1).start()
+        fetch(j).wait()
+        out_ref[:, j * LANES : (j + 1) * LANES] = contract(
+            q_ref[...], held_ref[j % slots], ((1,), (1,))
+        )
+
+
+def sum_kernel(parts_ref, out_ref):
+    share = parts_ref[0].astype(jnp.float32)
+    for j in range(1, parts_ref.shape[0]):
+        share = share + parts_ref[j].astype(jnp.float32)
+    share = share.astype(jnp.bfloat16)
+    for j in range(out_ref.shape[0]):
+        out_ref[j] = share
 
 
 def places(units):
@@ -203,13 +251,26 @@
     units = h_rows.shape[1]
     some = rank // parts
 
-    proj_local = jnp.dot(g_rows, q_prev, preferred_element_type=f32).astype(bf16)
-    first, proj_local = lax.optimization_barrier((lax.axis_index("core") == 0, proj_local))
-    proj = spread(proj_local.T, MP)
-    base = jnp.dot(e_rows, q_prev, preferred_element_type=f32).T
+    (copies,) = small_call(
+        project_kernel, [((parts, rank, LANES), bf16)], q_prev.T, g_rows, name="project"
+    )
+    first, copies, q_rows = lax.optimization_barrier(
+        (lax.axis_index("core") == 0, copies, q_prev.T)
+    )
+    proj = exchange(copies, MP)
+    (base,) = small_call(
+        base_kernel,
+        [((rank, units), f32)],
+        q_rows,
+        e_rows,
+        spaces=[pltpu.VMEM, pltpu.HBM],
+        scratch=[pltpu.VMEM((3, LANES, e_rows.shape[1]), bf16), pltpu.SemaphoreType.DMA((3,))],
+        name="base",
+    )
     p_terms = left_terms(proj, h_rows, base, groups)
-    p_part = total(exchange(p_terms, DP)).astype(bf16)
-    parts_of_mixed, p_sum = mixed_terms(spread(p_part, DP), h_rows, rank, units, parts)
+    p_terms = exchange(p_terms, DP)
+    (p_copies,) = small_call(sum_kernel, [(p_terms.shape, bf16)], p_terms, name="p_copies")
+    parts_of_mixed, p_sum = mixed_terms(exchange(p_copies, DP), h_rows, rank, units, parts)
     got = exchange(parts_of_mixed, MP)
     mixed = total(got[:, :rank]).astype(bf16)
     gram_rows = jnp.concatenate(halves(whole(total(got[:, rank : rank + some]))), axis=1)

time: 117 us -> 119 us (1.017)
  matrix products: 12.7 us -> 5.61 us
  Pallas kernels: 6.69 us -> 13 us
  starting transfers between devices: 23.7 us -> 26.7 us
  waiting for transfers between devices: 14.3 us -> 11.3 us
  local copies, waits for them, and re-layouts: 6.78 us -> 9.16 us
    dot_general x2 -> x0, matrix products: 7.13 us -> none  [the longest x1 5.61 us: on_device(): base = jnp.dot(e_rows, q_prev, preferred_element_type=f32).T]
    pallas_call x0 -> x3, Pallas kernels: none -> 6.28 us  [small_call(): pl.pallas_call(kernel, out_shape=[jax.ShapeDtypeStruct(shape, dtype) for...]
    unnamed x6 -> x14, local copies, waits for them, and re-layouts: 5.29 us -> 8.44 us
    all_to_all x3, waiting for transfers between devices: 13 us -> 9.97 us  [exchange(): return lax.all_to_all(parts, axis, split_axis=0, concat_axis=0, tiled=True)]
    all_to_all x3, starting transfers between devices: 19.5 us -> 22.5 us  [exchange(): return lax.all_to_all(parts, axis, split_axis=0, concat_axis=0, tiled=True)]
  transfers between devices with their start and end apart: 6 -> 6, of which waited for: 5 -> 4; matrix products, arithmetic and copies ran while one was open for 10% -> 5% of each run, Pallas kernels for 3% -> 7%
where the time goes in v4:
time: 119 us; the launch traced here: 118 us
  blocking collectives  50 us (42%)
  starting transfers between devices  26.7 us (22%)
  Pallas kernels  13 us (11%)
  waiting for transfers between devices  11.3 us (9%)
  local copies, waits for them, and re-layouts  9.16 us (8%)
  matrix products  5.61 us (5%)
  other arithmetic  1.35 us (1%)
    all_to_all x4, blocking collectives, exchange(): return lax.all_to_all(parts, axis, split_axis=0, concat_axis=0, tiled=True)  50 us
    all_to_all x3, starting transfers between devices, exchange(): return lax.all_to_all(parts, axis, split_axis=0, concat_axis=0, tiled=True)  22.5 us
    all_to_all x3, waiting for transfers between devices, exchange(): return lax.all_to_all(parts, axis, split_axis=0, concat_axis=0, tiled=True)  9.97 us
    unnamed x14, local copies, waits for them, and re-layouts  8.44 us
    pallas_call x3, Pallas kernels, small_call(): pl.pallas_call(kernel, out_shape=[jax.ShapeDtypeStruct(shape, dtype) for...  6.28 us
    dot_general x3, matrix products, contract(): lax.dot_general(left, right, (dims, ((), ())), preferred_element_type=jnp...  5.61 us
    ppermute x3, starting transfers between devices, swap(): return lax.ppermute(block, 'core', [(0, 1), (1, 0)])  4.14 us
    pallas_call x1, Pallas kernels, inverse_factor(): pl.pallas_call(eliminate, out_shape=[pair, pair], in_specs=[pl.BlockSpec(...  3.78 us
  transfers between devices with their start and end apart: 6, of which 4 were waited for; matrix products, arithmetic and copies ran while one was open for 5% of the time, Pallas kernels for 7%

profile of v4, /device:TPU:1, one launch (start us, length us, event | category | flops | bytes accessed | tf_op | source)
XLA Modules:
  0.0 117.9 jit_solution(394276004446577801)
XLA Ops:
  0.6 0.0 copy-start.3
  0.6 1.2 %copy-done.3 = bf16[1,128,4096]{2,1,0:T(8,128)(2,1)S(1)} copy-done((bf16[1,128,4096]{2,1,0:T(8,128)(2,1)S(1)}, bf16[1,128,4096]{2,1,0:T(8,128)(2,1)}, u32[]{:S(2)}) %copy-start.3) | copy-done | bytes 1048600
  1.9 0.0 copy-start.5
  1.9 1.0 copy-done.5
  2.9 1.2 %project.1 = bf16[16,64,128]{2,1,0:T(8,128)(2,1)} custom-call(bf16[64,4096]{1,0:T(8,128)(2,1)S(1)} %bitcast.36, bf16[128,4096]{1,0:T(8,128)(2,1)S(1)} %bitcast.35), custom_call_target="tpu_custom_call" | custom-call | flops 1000000000 | bytes 4194304 | tf_op jit(solution)/shard_map/project/pallas_call | solution.py:59
  4.1 8.4 %all-to-all-start = ((bf16[16,64,128]{2,1,0:T(8,128)(2,1)}), bf16[16,64,128]{2,1,0:T(8,128)(2,1)S(1)}, u32[]{:S(2)}, u32[]{:S(2)}) async-start(bf16[16,64,128]{2,1,0:T(8,128)(2,1)} %project.1), calls=%async_computation | async-start | bytes 524288 | tf_op jit(solution)/shard_map/all_to_all | solution.py:27
  12.5 0.0 copy-start
  12.6 3.1 %copy-done = bf16[1,896,4096]{2,1,0:T(8,128)(2,1)S(1)} copy-done((bf16[1,896,4096]{2,1,0:T(8,128)(2,1)S(1)}, bf16[1,896,4096]{2,1,0:T(8,128)(2,1)}, u32[]{:S(2)}) %copy-start) | copy-done | bytes 7340056
  15.7 0.0 copy-start.6
  15.7 1.0 copy-done.6
  16.7 5.1 %base.1.base_ref = f32[64,896]{1,0:T(8,128)S(1)} custom-call(bf16[64,4096]{1,0:T(8,128)(2,1)S(1)} %bitcast.37, bf16[896,4096]{1,0:T(8,128)(2,1)S(1)} %bitcast.32), custom_call_target="tpu_custom_call" | custom-call | flops 1000000000 | bytes 4194304 | tf_op jit(solution)/shard_map/base/pallas_call | solution.py:59
  21.8 0.0 all-to-all-done.proj_ref
  21.8 0.0 copy-start.1
  21.8 2.0 %copy-done.1 = bf16[1,2048,896]{2,1,0:T(8,128)(2,1)S(1)} copy-done((bf16[1,2048,896]{2,1,0:T(8,128)(2,1)S(1)}, bf16[1,2048,896]{2,1,0:T(8,128)(2,1)}, u32[]{:S(2)}) %copy-start.1) | copy-done | bytes 3670040
  23.8 0.0 copy-start.2
  23.8 0.7 left_terms.1
  24.6 17.0 %all_to_all.35.parts_ref = bf16[16,32,128]{2,1,0:T(8,128)(2,1)S(1)} all-to-all(bf16[16,32,128]{2,1,0:T(8,128)(2,1)S(1)} %left_terms.1), channel_id=1, replica_groups=mesh['z'=8,'ylo'=2,'yhi'=2,'x'=4,'core'=2] {'z','ylo'}, dimensions={0} | all-to-all | bytes 262144 | tf_op jit(solution)/shard_map/all_to_all | solution.py:27
  41.6 11.1 %all_to_all.36.parts_ref = bf16[16,32,128]{2,1,0:T(8,128)(2,1)S(1)} all-to-all(bf16[16,32,128]{2,1,0:T(8,128)(2,1)S(1)} %p_copies.1), channel_id=1, replica_groups=mesh['z'=8,'ylo'=2,'yhi'=2,'x'=4,'core'=2] {'z','ylo'}, dimensions={0} | all-to-all | bytes 262144 | tf_op jit(solution)/shard_map/all_to_all | solution.py:27
  52.7 0.0 copy-done.2
  52.7 2.0 %mixed_terms.1 = (bf16[16,72,128]{2,1,0:T(8,128)(2,1)}, bf16[64,896]{1,0:T(8,128)(2,1)S(1)}) custom-call(bf16[16,32,128]{2,1,0:T(8,128)(2,1)S(1)} %all_to_all.36.parts_ref, bf16[2048,896]{1,0:T(8,128)(2,1)S(1)} %bitcast.34), custom_call_target="tpu_custom_call" | custom-call | flops 1000000000 | bytes 4194304 | tf_op jit(solution)/shard_map/mixed_terms/pallas_call | solution.py:150
  54.8 0.0 copy-start.4
  54.8 10.7 %all-to-all-start.3 = ((bf16[16,72,128]{2,1,0:T(8,128)(2,1)}), bf16[16,72,128]{2,1,0:T(8,128)(2,1)S(1)}, u32[]{:S(2)}, u32[]{:S(2)}) async-start(bf16[16,72,128]{2,1,0:T(8,128)(2,1)} %get-tuple-element.15), calls=%async_computation.3 | async-start | bytes 589824 | tf_op jit(solution)/shard_map/all_to_all | solution.py:27
  65.5 4.5 %fusion.9 = f32[64,4096]{1,0:T(8,128)S(1)} fusion(bf16[64,896]{1,0:T(8,128)(2,1)S(1)} %get-tuple-element.13, bf16[1,896,4096]{2,1,0:T(8,128)(2,1)} %param.6), kind=kOutput, calls=%fused_computation.28 | convolution fusion | flops 469762048 | bytes 8503296 | tf_op jit(solution)/shard_map/dot_general | solution.py:23
  70.0 4.4 %all-to-all-done.3 = bf16[16,72,128]{2,1,0:T(8,128)(2,1)S(1)} async-done(((bf16[16,72,128]{2,1,0:T(8,128)(2,1)}), bf16[16,72,128]{2,1,0:T(8,128)(2,1)S(1)}, u32[]{:S(2)}, u32[]{:S(2)}) %all-to-all-start.3) | async-done | bytes 294944 | tf_op jit(solution)/shard_map/all_to_all | solution.py:27
  74.4 0.0 copy-done.4
  74.4 0.3 convolution_add_fusion
  74.7 0.1 select_convert_fusion
  74.8 1.0 collective-permute-start
  75.8 0.1 reduce-precision_convert_fusion
  75.9 0.1 fusion.7
  76.0 1.0 collective-permute-done
  76.9 0.1 bitcast_bitcast_fusion
  77.1 11.1 %all_to_all.37 = bf16[16,72,128]{2,1,0:T(8,128)(2,1)S(1)} all-to-all(bf16[16,72,128]{2,1,0:T(8,128)(2,1)S(1)} %pad_maximum_fusion), channel_id=1, replica_groups=mesh['z'=8,'ylo'=2,'yhi'=2,'x'=4,'core'=2] {'ylo','yhi','x'}, dimensions={0} | all-to-all | bytes 589824 | tf_op jit(solution)/shard_map/all_to_all | solution.py:27
  88.2 1.6 %collective-permute-start.1 = (bf16[8,8,128]{2,1,0:T(8,128)(2,1)S(1)}, bf16[8,8,128]{2,1,0:T(8,128)(2,1)S(1)}, u32[]{:S(2)}, u32[]{:S(2)}) collective-permute-start(bf16[8,8,128]{2,1,0:T(8,128)(2,1)S(1)} %slice.31), channel_id=1, source_target_pairs={{0,1},{1,0},{2,3},{3,2},{4,5},{5,4},{6,7},{7,6},{8,9},{9,8},{10,11... | collective-permute-start | bytes 49160 | tf_op jit(solution)/shard_map/ppermute | solution.py:36
  89.8 0.7 broadcast_in_dim.5
  90.5 3.4 %all-to-all-start.5 = ((bf16[8,64,128]{2,1,0:T(8,128)(2,1)}), bf16[8,64,128]{2,1,0:T(8,128)(2,1)S(1)}, u32[]{:S(2)}, u32[]{:S(2)}) async-start(bf16[8,64,128]{2,1,0:T(8,128)(2,1)} %broadcast_in_dim.5), calls=%async_computation.5 | async-start | bytes 262144 | tf_op jit(solution)/shard_map/all_to_all | solution.py:27
  93.8 0.0 collective-permute-done.1
  93.9 3.8 %inverse_factor.1 = (bf16[64,128]{1,0:T(8,128)(2,1)S(1)}, bf16[64,128]{1,0:T(8,128)(2,1)S(1)}) custom-call(bf16[8,8,128]{2,1,0:T(8,128)(2,1)S(1)} %get-tuple-element.23.zero_ref, bf16[8,8,128]{2,1,0:T(8,128)(2,1)S(1)} %get-tuple-element.22.one_ref), custom_call_target="tpu_custom_call" | custom-call | flops 4000000000 | bytes 49152 | tf_op jit(solution)/shard_map/inverse_factor/pallas_call | solution.py:207
  97.7 5.6 %all-to-all-done.5.parts_ref = bf16[8,64,128]{2,1,0:T(8,128)(2,1)S(1)} async-done(((bf16[8,64,128]{2,1,0:T(8,128)(2,1)}), bf16[8,64,128]{2,1,0:T(8,128)(2,1)S(1)}, u32[]{:S(2)}, u32[]{:S(2)}) %all-to-all-start.5) | async-done | bytes 131104 | tf_op jit(solution)/shard_map/all_to_all | solution.py:27
  103.2 0.2 scaled_copies.1
  103.4 10.8 %all_to_all.38 = bf16[16,64,128]{2,1,0:T(8,128)(2,1)S(1)} all-to-all(bf16[16,64,128]{2,1,0:T(8,128)(2,1)S(1)} %scaled_copies.1), channel_id=1, replica_groups=mesh['z'=8,'ylo'=2,'yhi'=2,'x'=4,'core'=2] {'ylo','yhi','x'}, dimensions={0} | all-to-all | bytes 524288 | tf_op jit(solution)/shard_map/all_to_all | solution.py:27
  114.2 1.6 %collective-permute-start.2 = (bf16[64,2048]{1,0:T(8,128)(2,1)S(1)}, bf16[64,2048]{1,0:T(8,128)(2,1)S(1)}, u32[]{:S(2)}, u32[]{:S(2)}) collective-permute-start(bf16[64,2048]{1,0:T(8,128)(2,1)S(1)} %copy_bitcast_fusion), channel_id=1, source_target_pairs={{0,1},{1,0},{2,3},{3,2},{4,5},{5,4},{6,7},{7,6},{8,9},{9,8},{10,11... | collective-permute-start | bytes 786440 | tf_op jit(solution)/shard_map/ppermute | solution.py:36
  115.8 0.8 convolution_convert_fusion
  116.6 0.3 collective-permute-done.2
  116.9 0.1 broadcast_select_fusion.1
  117.0 0.8 maximum_bitcast_fusion
  (9 shorter events, 0.2 us)
Async XLA Ops:
  0.6 1.2 %copy-start.3 = (bf16[1,128,4096]{2,1,0:T(8,128)(2,1)S(1)}, bf16[1,128,4096]{2,1,0:T(8,128)(2,1)}, u32[]{:S(2)}) copy-start(bf16[1,128,4096]{2,1,0:T(8,128)(2,1)} %param.4) | copy-start | bytes 3145732
  1.9 1.0 copy-start.5
  4.1 17.7 %all-to-all-start = ((bf16[16,64,128]{2,1,0:T(8,128)(2,1)}), bf16[16,64,128]{2,1,0:T(8,128)(2,1)S(1)}, u32[]{:S(2)}, u32[]{:S(2)}) async-start(bf16[16,64,128]{2,1,0:T(8,128)(2,1)} %project.1), calls=%async_computation | async-start | bytes 524288 | tf_op jit(solution)/shard_map/all_to_all | solution.py:27
  12.5 3.1 %copy-start = (bf16[1,896,4096]{2,1,0:T(8,128)(2,1)S(1)}, bf16[1,896,4096]{2,1,0:T(8,128)(2,1)}, u32[]{:S(2)}) copy-start(bf16[1,896,4096]{2,1,0:T(8,128)(2,1)} %param.6) | copy-start | bytes 22020100
  15.7 1.0 copy-start.6
  21.8 2.0 %copy-start.1 = (bf16[1,2048,896]{2,1,0:T(8,128)(2,1)S(1)}, bf16[1,2048,896]{2,1,0:T(8,128)(2,1)}, u32[]{:S(2)}) copy-start(bf16[1,2048,896]{2,1,0:T(8,128)(2,1)} %param.5) | copy-start | bytes 11010052
  23.8 28.9 %copy-start.2 = (bf16[1,2048,896]{2,1,0:T(8,128)(2,1)S(1)}, bf16[1,2048,896]{2,1,0:T(8,128)(2,1)}, u32[]{:S(2)}) copy-start(bf16[1,2048,896]{2,1,0:T(8,128)(2,1)} %param.5) | copy-start | bytes 11010052
  54.8 19.6 %copy-start.4 = (bf16[1,128,4096]{2,1,0:T(8,128)(2,1)S(1)}, bf16[1,128,4096]{2,1,0:T(8,128)(2,1)}, u32[]{:S(2)}) copy-start(bf16[1,128,4096]{2,1,0:T(8,128)(2,1)} %param.4) | copy-start | bytes 3145732
  54.8 19.6 %all-to-all-start.3 = ((bf16[16,72,128]{2,1,0:T(8,128)(2,1)}), bf16[16,72,128]{2,1,0:T(8,128)(2,1)S(1)}, u32[]{:S(2)}, u32[]{:S(2)}) async-start(bf16[16,72,128]{2,1,0:T(8,128)(2,1)} %get-tuple-element.15), calls=%async_computation.3 | async-start | bytes 589824 | tf_op jit(solution)/shard_map/all_to_all | solution.py:27
  74.8 2.2 %collective-permute-start = (bf16[64,2048]{1,0:T(8,128)(2,1)S(1)}, bf16[64,2048]{1,0:T(8,128)(2,1)S(1)}, u32[]{:S(2)}, u32[]{:S(2)}) collective-permute-start(bf16[64,2048]{1,0:T(8,128)(2,1)S(1)} %select_convert_fusion), channel_id=1, source_target_pairs={{0,1},{1,0},{2,3},{3,2},{4,5},{5,4},{6,7},{7,6},{8,9},{9,8},{10,11... | collective-permute-start | bytes 786440 | tf_op jit(solution)/shard_map/ppermute | solution.py:36
  88.2 5.6 %collective-permute-start.1 = (bf16[8,8,128]{2,1,0:T(8,128)(2,1)S(1)}, bf16[8,8,128]{2,1,0:T(8,128)(2,1)S(1)}, u32[]{:S(2)}, u32[]{:S(2)}) collective-permute-start(bf16[8,8,128]{2,1,0:T(8,128)(2,1)S(1)} %slice.31), channel_id=1, source_target_pairs={{0,1},{1,0},{2,3},{3,2},{4,5},{5,4},{6,7},{7,6},{8,9},{9,8},{10,11... | collective-permute-start | bytes 49160 | tf_op jit(solution)/shard_map/ppermute | solution.py:36
  90.5 12.8 %all-to-all-start.5 = ((bf16[8,64,128]{2,1,0:T(8,128)(2,1)}), bf16[8,64,128]{2,1,0:T(8,128)(2,1)S(1)}, u32[]{:S(2)}, u32[]{:S(2)}) async-start(bf16[8,64,128]{2,1,0:T(8,128)(2,1)} %broadcast_in_dim.5), calls=%async_computation.5 | async-start | bytes 262144 | tf_op jit(solution)/shard_map/all_to_all | solution.py:27
  114.2 2.7 %collective-permute-start.2 = (bf16[64,2048]{1,0:T(8,128)(2,1)S(1)}, bf16[64,2048]{1,0:T(8,128)(2,1)S(1)}, u32[]{:S(2)}, u32[]{:S(2)}) collective-permute-start(bf16[64,2048]{1,0:T(8,128)(2,1)S(1)} %copy_bitcast_fusion), channel_id=1, source_target_pairs={{0,1},{1,0},{2,3},{3,2},{4,5},{5,4},{6,7},{7,6},{8,9},{9,8},{10,11... | collective-permute-start | bytes 786440 | tf_op jit(solution)/shard_map/ppermute | solution.py:36

commit v5 on v3

--- a/solution.py
+++ b/solution.py
@@ -52,6 +52,27 @@
 
 def by_lanes(array, count):
     return array.reshape(array.shape[0], count, -1).transpose(1, 0, 2)
+
+
+def sum_kernel(parts_ref, out_ref):
+    share = parts_ref[0].astype(jnp.float32)
+    for j in range(1, parts_ref.shape[0]):
+        share = share + parts_ref[j].astype(jnp.float32)
+    share = share.astype(jnp.bfloat16)
+    for j in range(out_ref.shape[0]):
+        out_ref[j] = share
+
+
+def sum_copies(parts):
+    return pl.pallas_call(
+        sum_kernel,
+        out_shape=jax.ShapeDtypeStruct(parts.shape, parts.dtype),
+        in_specs=[pl.BlockSpec(memory_space=pltpu.VMEM)],
+        out_specs=pl.BlockSpec(memory_space=pltpu.VMEM),
+        cost_estimate=pl.CostEstimate(flops=65536, bytes_accessed=262144, transcendentals=0),
+        compiler_params=pltpu.CompilerParams(vmem_limit_bytes=VMEM_BYTES),
+        name="sum_copies",
+    )(parts)
 
 
 def places(units):
@@ -208,8 +229,8 @@
     proj = spread(proj_local.T, MP)
     base = jnp.dot(e_rows, q_prev, preferred_element_type=f32).T
     p_terms = left_terms(proj, h_rows, base, groups)
-    p_part = total(exchange(p_terms, DP)).astype(bf16)
-    parts_of_mixed, p_sum = mixed_terms(spread(p_part, DP), h_rows, rank, units, parts)
+    p_copies = sum_copies(exchange(p_terms, DP))
+    parts_of_mixed, p_sum = mixed_terms(exchange(p_copies, DP), h_rows, rank, units, parts)
     got = exchange(parts_of_mixed, MP)
     mixed = total(got[:, :rank]).astype(bf16)
     gram_rows = jnp.concatenate(halves(whole(total(got[:, rank : rank + some]))), axis=1)

time: 117 us -> 117 us (level)
  no operation moved by 1% of the time
where the time goes in v5:
time: 117 us; the launch traced here: 116 us
  blocking collectives  49.7 us (42%)
  starting transfers between devices  23.7 us (20%)
  waiting for transfers between devices  14.3 us (12%)
  matrix products  12.7 us (11%)
  local copies, waits for them, and re-layouts  6.76 us (6%)
  Pallas kernels  6.73 us (6%)
  other arithmetic  1.35 us (1%)
    all_to_all x4, blocking collectives, exchange(): return lax.all_to_all(parts, axis, split_axis=0, concat_axis=0, tiled=True)  49.7 us
    all_to_all x3, starting transfers between devices, exchange(): return lax.all_to_all(parts, axis, split_axis=0, concat_axis=0, tiled=True)  19.5 us
    all_to_all x3, waiting for transfers between devices, exchange(): return lax.all_to_all(parts, axis, split_axis=0, concat_axis=0, tiled=True)  13 us
    dot_general x3, matrix products, contract(): lax.dot_general(left, right, (dims, ((), ())), preferred_element_type=jnp...  5.62 us
    dot_general x1, matrix products, on_device(): base = jnp.dot(e_rows, q_prev, preferred_element_type=f32).T  5.61 us
    unnamed x6, local copies, waits for them, and re-layouts  5.29 us
    ppermute x3, starting transfers between devices, swap(): return lax.ppermute(block, 'core', [(0, 1), (1, 0)])  4.13 us
    pallas_call x1, Pallas kernels, inverse_factor(): pl.pallas_call(eliminate, out_shape=[pair, pair], in_specs=[pl.BlockSpec(...  3.78 us
  transfers between devices with their start and end apart: 6, of which 5 were waited for; matrix products, arithmetic and copies ran while one was open for 10% of the time, Pallas kernels for 3%

profile of v5, /device:TPU:1, one launch (start us, length us, event | category | flops | bytes accessed | tf_op | source)
XLA Modules:
  0.0 116.1 jit_solution(15165031261556539605)
XLA Ops:
  0.6 0.0 copy-start
  0.6 1.2 %copy-done = bf16[1,128,4096]{2,1,0:T(8,128)(2,1)S(1)} copy-done((bf16[1,128,4096]{2,1,0:T(8,128)(2,1)S(1)}, bf16[1,128,4096]{2,1,0:T(8,128)(2,1)}, u32[]{:S(2)}) %copy-start) | copy-done | bytes 1048600
  1.9 1.5 %convolution_convert_fusion.1 = bf16[128,64]{0,1:T(8,128)(2,1)S(1)} fusion(bf16[4096,64]{0,1:T(8,128)(2,1)} %param.7, bf16[1,128,4096]{2,1,0:T(8,128)(2,1)S(1)} %copy-done), kind=kOutput, calls=%fused_computation.6 | convolution fusion | flops 67117056 | bytes 1589248 | tf_op jit(solution)/shard_map/dot_general | solution.py:227
  3.4 0.8 broadcast_in_dim.6
  4.1 8.4 %all-to-all-start = ((bf16[16,64,128]{2,1,0:T(8,128)(2,1)}), bf16[16,64,128]{2,1,0:T(8,128)(2,1)S(1)}, u32[]{:S(2)}, u32[]{:S(2)}) async-start(bf16[16,64,128]{2,1,0:T(8,128)(2,1)} %broadcast_in_dim.6), calls=%async_computation | async-start | bytes 524288 | tf_op jit(solution)/shard_map/all_to_all | solution.py:27
  12.6 5.6 %fusion.2.base_ref = f32[64,896]{1,0:T(8,128)S(1)} fusion(bf16[4096,64]{0,1:T(8,128)(2,1)} %param.7, bf16[1,896,4096]{2,1,0:T(8,128)(2,1)} %param.6), kind=kOutput, calls=%fused_computation.2 | convolution fusion | flops 469762048 | bytes 8093696 | tf_op jit(solution)/shard_map/dot_general | solution.py:230
  18.2 3.1 %all-to-all-done.proj_ref = bf16[16,64,128]{2,1,0:T(8,128)(2,1)S(1)} async-done(((bf16[16,64,128]{2,1,0:T(8,128)(2,1)}), bf16[16,64,128]{2,1,0:T(8,128)(2,1)S(1)}, u32[]{:S(2)}, u32[]{:S(2)}) %all-to-all-start) | async-done | bytes 262176 | tf_op jit(solution)/shard_map/all_to_all | solution.py:27
  21.3 0.0 copy-start.1
  21.3 2.0 %copy-done.1 = bf16[1,2048,896]{2,1,0:T(8,128)(2,1)S(1)} copy-done((bf16[1,2048,896]{2,1,0:T(8,128)(2,1)S(1)}, bf16[1,2048,896]{2,1,0:T(8,128)(2,1)}, u32[]{:S(2)}) %copy-start.1) | copy-done | bytes 3670040
  23.3 0.7 left_terms.1
  24.0 16.7 %all_to_all.35.parts_ref = bf16[16,32,128]{2,1,0:T(8,128)(2,1)S(1)} all-to-all(bf16[16,32,128]{2,1,0:T(8,128)(2,1)S(1)} %left_terms.1), channel_id=1, replica_groups=mesh['z'=8,'ylo'=2,'yhi'=2,'x'=4,'core'=2] {'z','ylo'}, dimensions={0} | all-to-all | bytes 262144 | tf_op jit(solution)/shard_map/all_to_all | solution.py:27
  40.8 11.1 %all_to_all.36.parts_ref = bf16[16,32,128]{2,1,0:T(8,128)(2,1)S(1)} all-to-all(bf16[16,32,128]{2,1,0:T(8,128)(2,1)S(1)} %sum_copies.1), channel_id=1, replica_groups=mesh['z'=8,'ylo'=2,'yhi'=2,'x'=4,'core'=2] {'z','ylo'}, dimensions={0} | all-to-all | bytes 262144 | tf_op jit(solution)/shard_map/all_to_all | solution.py:27
  51.9 0.0 copy-start.2
  51.9 2.0 %copy-done.2 = bf16[1,2048,896]{2,1,0:T(8,128)(2,1)S(1)} copy-done((bf16[1,2048,896]{2,1,0:T(8,128)(2,1)S(1)}, bf16[1,2048,896]{2,1,0:T(8,128)(2,1)}, u32[]{:S(2)}) %copy-start.2) | copy-done | bytes 3670040
  53.9 2.0 %mixed_terms.1 = (bf16[16,72,128]{2,1,0:T(8,128)(2,1)}, bf16[64,896]{1,0:T(8,128)(2,1)S(1)}) custom-call(bf16[16,32,128]{2,1,0:T(8,128)(2,1)S(1)} %all_to_all.36.parts_ref, bf16[2048,896]{1,0:T(8,128)(2,1)S(1)} %bitcast.39), custom_call_target="tpu_custom_call" | custom-call | flops 1000000000 | bytes 4194304 | tf_op jit(solution)/shard_map/mixed_terms/pallas_call | solution.py:123
  56.0 7.7 %all-to-all-start.3 = ((bf16[16,72,128]{2,1,0:T(8,128)(2,1)}), bf16[16,72,128]{2,1,0:T(8,128)(2,1)S(1)}, u32[]{:S(2)}, u32[]{:S(2)}) async-start(bf16[16,72,128]{2,1,0:T(8,128)(2,1)} %get-tuple-element.13), calls=%async_computation.3 | async-start | bytes 589824 | tf_op jit(solution)/shard_map/all_to_all | solution.py:27
  63.7 4.5 %fusion = f32[64,4096]{1,0:T(8,128)S(1)} fusion(bf16[64,896]{1,0:T(8,128)(2,1)S(1)} %get-tuple-element.11, bf16[1,896,4096]{2,1,0:T(8,128)(2,1)} %param.6), kind=kOutput, calls=%fused_computation | convolution fusion | flops 469762048 | bytes 8503296 | tf_op jit(solution)/shard_map/dot_general | solution.py:23
  68.2 4.4 %all-to-all-done.3 = bf16[16,72,128]{2,1,0:T(8,128)(2,1)S(1)} async-done(((bf16[16,72,128]{2,1,0:T(8,128)(2,1)}), bf16[16,72,128]{2,1,0:T(8,128)(2,1)S(1)}, u32[]{:S(2)}, u32[]{:S(2)}) %all-to-all-start.3) | async-done | bytes 294944 | tf_op jit(solution)/shard_map/all_to_all | solution.py:27
  72.6 0.3 convolution_add_fusion
  72.9 0.1 select_convert_fusion
  73.0 1.0 collective-permute-start
  74.0 0.1 reduce-precision_convert_fusion
  74.1 0.1 fusion.13
  74.2 1.0 collective-permute-done
  75.1 0.1 bitcast_bitcast_fusion
  75.3 11.1 %all_to_all.37 = bf16[16,72,128]{2,1,0:T(8,128)(2,1)S(1)} all-to-all(bf16[16,72,128]{2,1,0:T(8,128)(2,1)S(1)} %pad_maximum_fusion), channel_id=1, replica_groups=mesh['z'=8,'ylo'=2,'yhi'=2,'x'=4,'core'=2] {'ylo','yhi','x'}, dimensions={0} | all-to-all | bytes 589824 | tf_op jit(solution)/shard_map/all_to_all | solution.py:27
  86.4 1.6 %collective-permute-start.1 = (bf16[8,8,128]{2,1,0:T(8,128)(2,1)S(1)}, bf16[8,8,128]{2,1,0:T(8,128)(2,1)S(1)}, u32[]{:S(2)}, u32[]{:S(2)}) collective-permute-start(bf16[8,8,128]{2,1,0:T(8,128)(2,1)S(1)} %slice.31), channel_id=1, source_target_pairs={{0,1},{1,0},{2,3},{3,2},{4,5},{5,4},{6,7},{7,6},{8,9},{9,8},{10,11... | collective-permute-start | bytes 49160 | tf_op jit(solution)/shard_map/ppermute | solution.py:36
  88.0 0.7 broadcast_in_dim.8
  88.7 3.4 %all-to-all-start.5 = ((bf16[8,64,128]{2,1,0:T(8,128)(2,1)}), bf16[8,64,128]{2,1,0:T(8,128)(2,1)S(1)}, u32[]{:S(2)}, u32[]{:S(2)}) async-start(bf16[8,64,128]{2,1,0:T(8,128)(2,1)} %broadcast_in_dim.8), calls=%async_computation.5 | async-start | bytes 262144 | tf_op jit(solution)/shard_map/all_to_all | solution.py:27
  92.0 0.0 collective-permute-done.1
  92.1 3.8 %inverse_factor.1 = (bf16[64,128]{1,0:T(8,128)(2,1)S(1)}, bf16[64,128]{1,0:T(8,128)(2,1)S(1)}) custom-call(bf16[8,8,128]{2,1,0:T(8,128)(2,1)S(1)} %get-tuple-element.21.zero_ref, bf16[8,8,128]{2,1,0:T(8,128)(2,1)S(1)} %get-tuple-element.20.one_ref), custom_call_target="tpu_custom_call" | custom-call | flops 4000000000 | bytes 49152 | tf_op jit(solution)/shard_map/inverse_factor/pallas_call | solution.py:180
  95.8 5.6 %all-to-all-done.5.parts_ref = bf16[8,64,128]{2,1,0:T(8,128)(2,1)S(1)} async-done(((bf16[8,64,128]{2,1,0:T(8,128)(2,1)}), bf16[8,64,128]{2,1,0:T(8,128)(2,1)S(1)}, u32[]{:S(2)}, u32[]{:S(2)}) %all-to-all-start.5) | async-done | bytes 131104 | tf_op jit(solution)/shard_map/all_to_all | solution.py:27
  101.4 0.2 scaled_copies.1
  101.6 10.8 %all_to_all.38 = bf16[16,64,128]{2,1,0:T(8,128)(2,1)S(1)} all-to-all(bf16[16,64,128]{2,1,0:T(8,128)(2,1)S(1)} %scaled_copies.1), channel_id=1, replica_groups=mesh['z'=8,'ylo'=2,'yhi'=2,'x'=4,'core'=2] {'ylo','yhi','x'}, dimensions={0} | all-to-all | bytes 524288 | tf_op jit(solution)/shard_map/all_to_all | solution.py:27
  112.4 1.6 %collective-permute-start.2 = (bf16[64,2048]{1,0:T(8,128)(2,1)S(1)}, bf16[64,2048]{1,0:T(8,128)(2,1)S(1)}, u32[]{:S(2)}, u32[]{:S(2)}) collective-permute-start(bf16[64,2048]{1,0:T(8,128)(2,1)S(1)} %copy_bitcast_fusion), channel_id=1, source_target_pairs={{0,1},{1,0},{2,3},{3,2},{4,5},{5,4},{6,7},{7,6},{8,9},{9,8},{10,11... | collective-permute-start | bytes 786440 | tf_op jit(solution)/shard_map/ppermute | solution.py:36
  114.0 0.8 convolution_convert_fusion
  114.8 0.3 collective-permute-done.2
  115.1 0.1 broadcast_select_fusion.1
  115.2 0.8 maximum_bitcast_fusion
  (9 shorter events, 0.2 us)
Async XLA Ops:
  0.6 1.2 %copy-start = (bf16[1,128,4096]{2,1,0:T(8,128)(2,1)S(1)}, bf16[1,128,4096]{2,1,0:T(8,128)(2,1)}, u32[]{:S(2)}) copy-start(bf16[1,128,4096]{2,1,0:T(8,128)(2,1)} %param.4) | copy-start | bytes 3145732
  4.1 17.1 %all-to-all-start = ((bf16[16,64,128]{2,1,0:T(8,128)(2,1)}), bf16[16,64,128]{2,1,0:T(8,128)(2,1)S(1)}, u32[]{:S(2)}, u32[]{:S(2)}) async-start(bf16[16,64,128]{2,1,0:T(8,128)(2,1)} %broadcast_in_dim.6), calls=%async_computation | async-start | bytes 524288 | tf_op jit(solution)/shard_map/all_to_all | solution.py:27
  21.3 2.0 %copy-start.1 = (bf16[1,2048,896]{2,1,0:T(8,128)(2,1)S(1)}, bf16[1,2048,896]{2,1,0:T(8,128)(2,1)}, u32[]{:S(2)}) copy-start(bf16[1,2048,896]{2,1,0:T(8,128)(2,1)} %param.5) | copy-start | bytes 11010052
  51.9 2.0 %copy-start.2 = (bf16[1,2048,896]{2,1,0:T(8,128)(2,1)S(1)}, bf16[1,2048,896]{2,1,0:T(8,128)(2,1)}, u32[]{:S(2)}) copy-start(bf16[1,2048,896]{2,1,0:T(8,128)(2,1)} %param.5) | copy-start | bytes 11010052
  56.0 16.6 %all-to-all-start.3 = ((bf16[16,72,128]{2,1,0:T(8,128)(2,1)}), bf16[16,72,128]{2,1,0:T(8,128)(2,1)S(1)}, u32[]{:S(2)}, u32[]{:S(2)}) async-start(bf16[16,72,128]{2,1,0:T(8,128)(2,1)} %get-tuple-element.13), calls=%async_computation.3 | async-start | bytes 589824 | tf_op jit(solution)/shard_map/all_to_all | solution.py:27
  73.0 2.2 %collective-permute-start = (bf16[64,2048]{1,0:T(8,128)(2,1)S(1)}, bf16[64,2048]{1,0:T(8,128)(2,1)S(1)}, u32[]{:S(2)}, u32[]{:S(2)}) collective-permute-start(bf16[64,2048]{1,0:T(8,128)(2,1)S(1)} %select_convert_fusion), channel_id=1, source_target_pairs={{0,1},{1,0},{2,3},{3,2},{4,5},{5,4},{6,7},{7,6},{8,9},{9,8},{10,11... | collective-permute-start | bytes 786440 | tf_op jit(solution)/shard_map/ppermute | solution.py:36
  86.4 5.6 %collective-permute-start.1 = (bf16[8,8,128]{2,1,0:T(8,128)(2,1)S(1)}, bf16[8,8,128]{2,1,0:T(8,128)(2,1)S(1)}, u32[]{:S(2)}, u32[]{:S(2)}) collective-permute-start(bf16[8,8,128]{2,1,0:T(8,128)(2,1)S(1)} %slice.31), channel_id=1, source_target_pairs={{0,1},{1,0},{2,3},{3,2},{4,5},{5,4},{6,7},{7,6},{8,9},{9,8},{10,11... | collective-permute-start | bytes 49160 | tf_op jit(solution)/shard_map/ppermute | solution.py:36
  88.7 12.8 %all-to-all-start.5 = ((bf16[8,64,128]{2,1,0:T(8,128)(2,1)}), bf16[8,64,128]{2,1,0:T(8,128)(2,1)S(1)}, u32[]{:S(2)}, u32[]{:S(2)}) async-start(bf16[8,64,128]{2,1,0:T(8,128)(2,1)} %broadcast_in_dim.8), calls=%async_computation.5 | async-start | bytes 262144 | tf_op jit(solution)/shard_map/all_to_all | solution.py:27
  112.4 2.7 %collective-permute-start.2 = (bf16[64,2048]{1,0:T(8,128)(2,1)S(1)}, bf16[64,2048]{1,0:T(8,128)(2,1)S(1)}, u32[]{:S(2)}, u32[]{:S(2)}) collective-permute-start(bf16[64,2048]{1,0:T(8,128)(2,1)S(1)} %copy_bitcast_fusion), channel_id=1, source_target_pairs={{0,1},{1,0},{2,3},{3,2},{4,5},{5,4},{6,7},{7,6},{8,9},{9,8},{10,11... | collective-permute-start | bytes 786440 | tf_op jit(solution)/shard_map/ppermute | solution.py:36

commit v6 on v5

--- a/solution.py
+++ b/solution.py
@@ -11,6 +11,7 @@
 FF = 14336
 GROUPS = 16
 VMEM_BYTES = 4 << 20
+LEFT_BYTES = 54 << 20
 ROWS, LANES = 32, 128
 AXES = ("z", "ylo", "yhi", "x", "core")
 SIZES = (-1, 2, 2, 4, 2)
@@ -79,9 +80,22 @@
     return [(r, c) for r in (0, ROWS) for c in range(0, units, LANES)]
 
 
-def left_kernel(proj_ref, h_ref, base_ref, out_ref):
-    proj = jnp.concatenate([proj_ref[j] for j in range(proj_ref.shape[0])], axis=1)
-    terms = base_ref[...] + contract(proj, h_ref[...], ((1,), (0,)))
+def left_kernel(proj_ref, h_ref, base_ref, out_ref, held_ref, arrived):
+    blocks = arrived.shape[0]
+    rows = h_ref.shape[0] // blocks
+    near = rows // LANES
+
+    def fetch(j):
+        at = pl.ds(j * rows, rows)
+        return pltpu.make_async_copy(h_ref.at[at], held_ref.at[at], arrived.at[j])
+
+    for j in range(blocks):
+        fetch(j).start()
+    terms = base_ref[...]
+    for j in range(blocks):
+        proj = jnp.concatenate([proj_ref[near * j + i] for i in range(near)], axis=1)
+        fetch(j).wait()
+        terms = terms + contract(proj, held_ref[j * rows : (j + 1) * rows], ((1,), (0,)))
     terms = terms.astype(jnp.bfloat16)
     used = places(terms.shape[1])
     for j, (r, c) in enumerate(used):
@@ -93,11 +107,19 @@
 def left_terms(proj, h_rows, base, count):
     return pl.pallas_call(
         left_kernel,
-        out_shape=jax.ShapeDtypeStruct((count, ROWS, LANES), jnp.bfloat16),
-        in_specs=[pl.BlockSpec(memory_space=pltpu.VMEM)] * 3,
-        out_specs=pl.BlockSpec(memory_space=pltpu.VMEM),
+        out_shape=[
+            jax.ShapeDtypeStruct((count, ROWS, LANES), jnp.bfloat16),
+            jax.ShapeDtypeStruct(h_rows.shape, h_rows.dtype),
+        ],
+        in_specs=[
+            pl.BlockSpec(memory_space=pltpu.VMEM),
+            pl.BlockSpec(memory_space=pltpu.HBM),
+            pl.BlockSpec(memory_space=pltpu.VMEM),
+        ],
+        out_specs=[pl.BlockSpec(memory_space=pltpu.VMEM)] * 2,
+        scratch_shapes=[pltpu.SemaphoreType.DMA((4,))],
         cost_estimate=pl.CostEstimate(flops=1_000_000_000, bytes_accessed=4 << 20, transcendentals=0),
-        compiler_params=pltpu.CompilerParams(vmem_limit_bytes=3 * VMEM_BYTES),
+        compiler_params=pltpu.CompilerParams(vmem_limit_bytes=LEFT_BYTES),
         name="left_terms",
     )(proj, h_rows, base)
 
@@ -228,9 +250,9 @@
     first, proj_local = lax.optimization_barrier((lax.axis_index("core") == 0, proj_local))
     proj = spread(proj_local.T, MP)
     base = jnp.dot(e_rows, q_prev, preferred_element_type=f32).T
-    p_terms = left_terms(proj, h_rows, base, groups)
+    p_terms, h_held = left_terms(proj, h_rows, base, groups)
     p_copies = sum_copies(exchange(p_terms, DP))
-    parts_of_mixed, p_sum = mixed_terms(exchange(p_copies, DP), h_rows, rank, units, parts)
+    parts_of_mixed, p_sum = mixed_terms(exchange(p_copies, DP), h_held, rank, units, parts)
     got = exchange(parts_of_mixed, MP)
     mixed = total(got[:, :rank]).astype(bf16)
     gram_rows = jnp.concatenate(halves(whole(total(got[:, rank : rank + some]))), axis=1)

time: 117 us -> 120 us (1.026)
  Pallas kernels: 6.73 us -> 10.9 us
  local copies, waits for them, and re-layouts: 6.76 us -> 5.42 us
    pallas_call x1, Pallas kernels: 0.73 us -> 4.89 us  [left_terms(): pl.pallas_call(left_kernel, out_shape=[jax.ShapeDtypeStruct((count, ROWS,...]
    unnamed x6, local copies, waits for them, and re-layouts: 5.29 us -> 3.96 us
where the time goes in v6:
time: 120 us
  blocking collectives  49.9 us (42%)
  starting transfers between devices  24.1 us (20%)
  waiting for transfers between devices  13.7 us (11%)
  matrix products  13.4 us (11%)
  Pallas kernels  10.9 us (9%)
  local copies, waits for them, and re-layouts  5.42 us (5%)
  other arithmetic  1.35 us (1%)
    all_to_all x4, blocking collectives, exchange(): return lax.all_to_all(parts, axis, split_axis=0, concat_axis=0, tiled=True)  49.9 us
    all_to_all x3, starting transfers between devices, exchange(): return lax.all_to_all(parts, axis, split_axis=0, concat_axis=0, tiled=True)  20 us
    all_to_all x3, waiting for transfers between devices, exchange(): return lax.all_to_all(parts, axis, split_axis=0, concat_axis=0, tiled=True)  12.3 us
    dot_general x1, matrix products, on_device(): base = jnp.dot(e_rows, q_prev, preferred_element_type=f32).T  6.3 us
    dot_general x3, matrix products, contract(): lax.dot_general(left, right, (dims, ((), ())), preferred_element_type=jnp...  5.62 us
    pallas_call x1, Pallas kernels, left_terms(): pl.pallas_call(left_kernel, out_shape=[jax.ShapeDtypeStruct((count, ROWS,...  4.89 us
    ppermute x3, starting transfers between devices, swap(): return lax.ppermute(block, 'core', [(0, 1), (1, 0)])  4.13 us
    unnamed x6, local copies, waits for them, and re-layouts  3.96 us
  transfers between devices with their start and end apart: 6, of which 5 were waited for; matrix products, arithmetic and copies ran while one was open for 10% of the time, Pallas kernels for 3%

profile of v6, /device:TPU:1, one launch (start us, length us, event | category | flops | bytes accessed | tf_op | source)
XLA Modules:
  0.0 119.6 jit_solution(9103663888446480967)
XLA Ops:
  0.6 0.0 copy-start
  0.6 1.2 %copy-done = bf16[1,128,4096]{2,1,0:T(8,128)(2,1)S(1)} copy-done((bf16[1,128,4096]{2,1,0:T(8,128)(2,1)S(1)}, bf16[1,128,4096]{2,1,0:T(8,128)(2,1)}, u32[]{:S(2)}) %copy-start) | copy-done | bytes 1048600
  1.9 1.5 %convolution_convert_fusion.1 = bf16[128,64]{0,1:T(8,128)(2,1)S(1)} fusion(bf16[4096,64]{0,1:T(8,128)(2,1)} %param.7, bf16[1,128,4096]{2,1,0:T(8,128)(2,1)S(1)} %copy-done), kind=kOutput, calls=%fused_computation.6 | convolution fusion | flops 67117056 | bytes 1589248 | tf_op jit(solution)/shard_map/dot_general | solution.py:249
  3.4 0.8 broadcast_in_dim.6
  4.1 8.4 %all-to-all-start = ((bf16[16,64,128]{2,1,0:T(8,128)(2,1)}), bf16[16,64,128]{2,1,0:T(8,128)(2,1)S(1)}, u32[]{:S(2)}, u32[]{:S(2)}) async-start(bf16[16,64,128]{2,1,0:T(8,128)(2,1)} %broadcast_in_dim.6), calls=%async_computation | async-start | bytes 524288 | tf_op jit(solution)/shard_map/all_to_all | solution.py:28
  12.6 6.3 %fusion.2.base_ref = f32[64,896]{1,0:T(8,128)} fusion(bf16[4096,64]{0,1:T(8,128)(2,1)} %param.7, bf16[1,896,4096]{2,1,0:T(8,128)(2,1)} %param.6), kind=kOutput, calls=%fused_computation.2 | convolution fusion | flops 469762048 | bytes 8093696 | tf_op jit(solution)/shard_map/dot_general | solution.py:252
  18.9 2.4 %all-to-all-done.proj_ref = bf16[16,64,128]{2,1,0:T(8,128)(2,1)S(1)} async-done(((bf16[16,64,128]{2,1,0:T(8,128)(2,1)}), bf16[16,64,128]{2,1,0:T(8,128)(2,1)S(1)}, u32[]{:S(2)}, u32[]{:S(2)}) %all-to-all-start) | async-done | bytes 262176 | tf_op jit(solution)/shard_map/all_to_all | solution.py:28
  21.3 0.0 copy-start.2
  21.3 0.7 copy-done.2
  22.0 4.9 %left_terms.1 = (bf16[16,32,128]{2,1,0:T(8,128)(2,1)}, bf16[2048,896]{1,0:T(8,128)(2,1)}) custom-call(bf16[16,64,128]{2,1,0:T(8,128)(2,1)} %copy-done.2, bf16[2048,896]{1,0:T(8,128)(2,1)} %bitcast.38, f32[64,896]{1,0:T(8,128)} %fusion.2.base_ref), custom_call_target="tpu_custom_call" | custom-call | flops 1000000000 | bytes 4194304 | tf_op jit(solution)/shard_map/left_terms/pallas_call | solution.py:108
  26.9 16.9 %all_to_all.35.parts_ref = bf16[16,32,128]{2,1,0:T(8,128)(2,1)S(1)} all-to-all(bf16[16,32,128]{2,1,0:T(8,128)(2,1)} %get-tuple-element.13), channel_id=1, replica_groups=mesh['z'=8,'ylo'=2,'yhi'=2,'x'=4,'core'=2] {'z','ylo'}, dimensions={0} | all-to-all | bytes 262144 | tf_op jit(solution)/shard_map/all_to_all | solution.py:28
  43.8 11.1 %all_to_all.36.parts_ref = bf16[16,32,128]{2,1,0:T(8,128)(2,1)S(1)} all-to-all(bf16[16,32,128]{2,1,0:T(8,128)(2,1)S(1)} %sum_copies.1), channel_id=1, replica_groups=mesh['z'=8,'ylo'=2,'yhi'=2,'x'=4,'core'=2] {'z','ylo'}, dimensions={0} | all-to-all | bytes 262144 | tf_op jit(solution)/shard_map/all_to_all | solution.py:28
  54.9 0.0 copy-start.1
  54.9 2.0 %copy-done.1 = bf16[2048,896]{1,0:T(8,128)(2,1)S(1)} copy-done((bf16[2048,896]{1,0:T(8,128)(2,1)S(1)}, bf16[2048,896]{1,0:T(8,128)(2,1)}, u32[]{:S(2)}) %copy-start.1) | copy-done | bytes 3670040
  57.0 2.0 %mixed_terms.1 = (bf16[16,72,128]{2,1,0:T(8,128)(2,1)}, bf16[64,896]{1,0:T(8,128)(2,1)S(1)}) custom-call(bf16[16,32,128]{2,1,0:T(8,128)(2,1)S(1)} %all_to_all.36.parts_ref, bf16[2048,896]{1,0:T(8,128)(2,1)S(1)} %copy-done.1), custom_call_target="tpu_custom_call" | custom-call | flops 1000000000 | bytes 4194304 | tf_op jit(solution)/shard_map/mixed_terms/pallas_call | solution.py:145
  59.0 8.2 %all-to-all-start.3 = ((bf16[16,72,128]{2,1,0:T(8,128)(2,1)}), bf16[16,72,128]{2,1,0:T(8,128)(2,1)S(1)}, u32[]{:S(2)}, u32[]{:S(2)}) async-start(bf16[16,72,128]{2,1,0:T(8,128)(2,1)} %get-tuple-element.17), calls=%async_computation.3 | async-start | bytes 589824 | tf_op jit(solution)/shard_map/all_to_all | solution.py:28
  67.2 4.5 %fusion = f32[64,4096]{1,0:T(8,128)S(1)} fusion(bf16[64,896]{1,0:T(8,128)(2,1)S(1)} %get-tuple-element.15, bf16[1,896,4096]{2,1,0:T(8,128)(2,1)} %param.6), kind=kOutput, calls=%fused_computation | convolution fusion | flops 469762048 | bytes 8503296 | tf_op jit(solution)/shard_map/dot_general | solution.py:24
  71.7 4.4 %all-to-all-done.3 = bf16[16,72,128]{2,1,0:T(8,128)(2,1)S(1)} async-done(((bf16[16,72,128]{2,1,0:T(8,128)(2,1)}), bf16[16,72,128]{2,1,0:T(8,128)(2,1)S(1)}, u32[]{:S(2)}, u32[]{:S(2)}) %all-to-all-start.3) | async-done | bytes 294944 | tf_op jit(solution)/shard_map/all_to_all | solution.py:28
  76.1 0.3 convolution_add_fusion
  76.4 0.1 select_convert_fusion
  76.5 1.0 collective-permute-start
  77.5 0.1 reduce-precision_convert_fusion
  77.6 0.1 fusion.13
  77.7 1.0 collective-permute-done
  78.6 0.1 bitcast_bitcast_fusion
  78.8 11.1 %all_to_all.37 = bf16[16,72,128]{2,1,0:T(8,128)(2,1)S(1)} all-to-all(bf16[16,72,128]{2,1,0:T(8,128)(2,1)S(1)} %pad_maximum_fusion), channel_id=1, replica_groups=mesh['z'=8,'ylo'=2,'yhi'=2,'x'=4,'core'=2] {'ylo','yhi','x'}, dimensions={0} | all-to-all | bytes 589824 | tf_op jit(solution)/shard_map/all_to_all | solution.py:28
  89.9 1.6 %collective-permute-start.1 = (bf16[8,8,128]{2,1,0:T(8,128)(2,1)S(1)}, bf16[8,8,128]{2,1,0:T(8,128)(2,1)S(1)}, u32[]{:S(2)}, u32[]{:S(2)}) collective-permute-start(bf16[8,8,128]{2,1,0:T(8,128)(2,1)S(1)} %slice.31), channel_id=1, source_target_pairs={{0,1},{1,0},{2,3},{3,2},{4,5},{5,4},{6,7},{7,6},{8,9},{9,8},{10,11... | collective-permute-start | bytes 49160 | tf_op jit(solution)/shard_map/ppermute | solution.py:37
  91.5 0.7 broadcast_in_dim.8
  92.2 3.4 %all-to-all-start.5 = ((bf16[8,64,128]{2,1,0:T(8,128)(2,1)}), bf16[8,64,128]{2,1,0:T(8,128)(2,1)S(1)}, u32[]{:S(2)}, u32[]{:S(2)}) async-start(bf16[8,64,128]{2,1,0:T(8,128)(2,1)} %broadcast_in_dim.8), calls=%async_computation.5 | async-start | bytes 262144 | tf_op jit(solution)/shard_map/all_to_all | solution.py:28
  95.6 0.0 collective-permute-done.1
  95.6 3.8 %inverse_factor.1 = (bf16[64,128]{1,0:T(8,128)(2,1)S(1)}, bf16[64,128]{1,0:T(8,128)(2,1)S(1)}) custom-call(bf16[8,8,128]{2,1,0:T(8,128)(2,1)S(1)} %get-tuple-element.25.zero_ref, bf16[8,8,128]{2,1,0:T(8,128)(2,1)S(1)} %get-tuple-element.24.one_ref), custom_call_target="tpu_custom_call" | custom-call | flops 4000000000 | bytes 49152 | tf_op jit(solution)/shard_map/inverse_factor/pallas_call | solution.py:202
  99.4 5.6 %all-to-all-done.5.parts_ref = bf16[8,64,128]{2,1,0:T(8,128)(2,1)S(1)} async-done(((bf16[8,64,128]{2,1,0:T(8,128)(2,1)}), bf16[8,64,128]{2,1,0:T(8,128)(2,1)S(1)}, u32[]{:S(2)}, u32[]{:S(2)}) %all-to-all-start.5) | async-done | bytes 131104 | tf_op jit(solution)/shard_map/all_to_all | solution.py:28
  104.9 0.2 scaled_copies.1
  105.1 10.8 %all_to_all.38 = bf16[16,64,128]{2,1,0:T(8,128)(2,1)S(1)} all-to-all(bf16[16,64,128]{2,1,0:T(8,128)(2,1)S(1)} %scaled_copies.1), channel_id=1, replica_groups=mesh['z'=8,'ylo'=2,'yhi'=2,'x'=4,'core'=2] {'ylo','yhi','x'}, dimensions={0} | all-to-all | bytes 524288 | tf_op jit(solution)/shard_map/all_to_all | solution.py:28
  115.9 1.6 %collective-permute-start.2 = (bf16[64,2048]{1,0:T(8,128)(2,1)S(1)}, bf16[64,2048]{1,0:T(8,128)(2,1)S(1)}, u32[]{:S(2)}, u32[]{:S(2)}) collective-permute-start(bf16[64,2048]{1,0:T(8,128)(2,1)S(1)} %copy_bitcast_fusion), channel_id=1, source_target_pairs={{0,1},{1,0},{2,3},{3,2},{4,5},{5,4},{6,7},{7,6},{8,9},{9,8},{10,11... | collective-permute-start | bytes 786440 | tf_op jit(solution)/shard_map/ppermute | solution.py:37
  117.5 0.8 convolution_convert_fusion
  118.3 0.3 collective-permute-done.2
  118.6 0.1 broadcast_select_fusion.1
  118.7 0.8 maximum_bitcast_fusion
  (9 shorter events, 0.2 us)
Async XLA Ops:
  0.6 1.2 %copy-start = (bf16[1,128,4096]{2,1,0:T(8,128)(2,1)S(1)}, bf16[1,128,4096]{2,1,0:T(8,128)(2,1)}, u32[]{:S(2)}) copy-start(bf16[1,128,4096]{2,1,0:T(8,128)(2,1)} %param.4) | copy-start | bytes 3145732
  4.1 17.1 %all-to-all-start = ((bf16[16,64,128]{2,1,0:T(8,128)(2,1)}), bf16[16,64,128]{2,1,0:T(8,128)(2,1)S(1)}, u32[]{:S(2)}, u32[]{:S(2)}) async-start(bf16[16,64,128]{2,1,0:T(8,128)(2,1)} %broadcast_in_dim.6), calls=%async_computation | async-start | bytes 524288 | tf_op jit(solution)/shard_map/all_to_all | solution.py:28
  21.3 0.7 copy-start.2
  54.9 2.0 %copy-start.1 = (bf16[2048,896]{1,0:T(8,128)(2,1)S(1)}, bf16[2048,896]{1,0:T(8,128)(2,1)}, u32[]{:S(2)}) copy-start(bf16[2048,896]{1,0:T(8,128)(2,1)} %get-tuple-element.14.h_ref) | copy-start | bytes 11010052
  59.0 17.1 %all-to-all-start.3 = ((bf16[16,72,128]{2,1,0:T(8,128)(2,1)}), bf16[16,72,128]{2,1,0:T(8,128)(2,1)S(1)}, u32[]{:S(2)}, u32[]{:S(2)}) async-start(bf16[16,72,128]{2,1,0:T(8,128)(2,1)} %get-tuple-element.17), calls=%async_computation.3 | async-start | bytes 589824 | tf_op jit(solution)/shard_map/all_to_all | solution.py:28
  76.5 2.2 %collective-permute-start = (bf16[64,2048]{1,0:T(8,128)(2,1)S(1)}, bf16[64,2048]{1,0:T(8,128)(2,1)S(1)}, u32[]{:S(2)}, u32[]{:S(2)}) collective-permute-start(bf16[64,2048]{1,0:T(8,128)(2,1)S(1)} %select_convert_fusion), channel_id=1, source_target_pairs={{0,1},{1,0},{2,3},{3,2},{4,5},{5,4},{6,7},{7,6},{8,9},{9,8},{10,11... | collective-permute-start | bytes 786440 | tf_op jit(solution)/shard_map/ppermute | solution.py:37
  89.9 5.6 %collective-permute-start.1 = (bf16[8,8,128]{2,1,0:T(8,128)(2,1)S(1)}, bf16[8,8,128]{2,1,0:T(8,128)(2,1)S(1)}, u32[]{:S(2)}, u32[]{:S(2)}) collective-permute-start(bf16[8,8,128]{2,1,0:T(8,128)(2,1)S(1)} %slice.31), channel_id=1, source_target_pairs={{0,1},{1,0},{2,3},{3,2},{4,5},{5,4},{6,7},{7,6},{8,9},{9,8},{10,11... | collective-permute-start | bytes 49160 | tf_op jit(solution)/shard_map/ppermute | solution.py:37
  92.2 12.8 %all-to-all-start.5 = ((bf16[8,64,128]{2,1,0:T(8,128)(2,1)}), bf16[8,64,128]{2,1,0:T(8,128)(2,1)S(1)}, u32[]{:S(2)}, u32[]{:S(2)}) async-start(bf16[8,64,128]{2,1,0:T(8,128)(2,1)} %broadcast_in_dim.8), calls=%async_computation.5 | async-start | bytes 262144 | tf_op jit(solution)/shard_map/all_to_all | solution.py:28
  115.9 2.7 %collective-permute-start.2 = (bf16[64,2048]{1,0:T(8,128)(2,1)S(1)}, bf16[64,2048]{1,0:T(8,128)(2,1)S(1)}, u32[]{:S(2)}, u32[]{:S(2)}) collective-permute-start(bf16[64,2048]{1,0:T(8,128)(2,1)S(1)} %copy_bitcast_fusion), channel_id=1, source_target_pairs={{0,1},{1,0},{2,3},{3,2},{4,5},{5,4},{6,7},{7,6},{8,9},{9,8},{10,11... | collective-permute-start | bytes 786440 | tf_op jit(solution)/shard_map/ppermute | solution.py:37

commit v7 on v6

--- a/solution.py
+++ b/solution.py
@@ -11,7 +11,7 @@
 FF = 14336
 GROUPS = 16
 VMEM_BYTES = 4 << 20
-LEFT_BYTES = 54 << 20
+LEFT_BYTES = 50 << 20
 ROWS, LANES = 32, 128
 AXES = ("z", "ylo", "yhi", "x", "core")
 SIZES = (-1, 2, 2, 4, 2)

time: 120 us -> 118 us (0.983)
    unnamed x6 -> x4, local copies, waits for them, and re-layouts: 3.96 us -> 3.26 us
where the time goes in v7:
time: 118 us; the launch traced here: 117 us
  blocking collectives  49.7 us (42%)
  starting transfers between devices  23.7 us (20%)
  waiting for transfers between devices  14.3 us (12%)
  matrix products  12.7 us (11%)
  Pallas kernels  9.82 us (8%)
  local copies, waits for them, and re-layouts  4.72 us (4%)
  other arithmetic  1.35 us (1%)
    all_to_all x4, blocking collectives, exchange(): return lax.all_to_all(parts, axis, split_axis=0, concat_axis=0, tiled=True)  49.7 us
    all_to_all x3, starting transfers between devices, exchange(): return lax.all_to_all(parts, axis, split_axis=0, concat_axis=0, tiled=True)  19.5 us
    all_to_all x3, waiting for transfers between devices, exchange(): return lax.all_to_all(parts, axis, split_axis=0, concat_axis=0, tiled=True)  13 us
    dot_general x3, matrix products, contract(): lax.dot_general(left, right, (dims, ((), ())), preferred_element_type=jnp...  5.62 us
    dot_general x1, matrix products, on_device(): base = jnp.dot(e_rows, q_prev, preferred_element_type=f32).T  5.61 us
    ppermute x3, starting transfers between devices, swap(): return lax.ppermute(block, 'core', [(0, 1), (1, 0)])  4.13 us
    pallas_call x1, Pallas kernels, left_terms(): pl.pallas_call(left_kernel, out_shape=[jax.ShapeDtypeStruct((count, ROWS,...  3.84 us
    pallas_call x1, Pallas kernels, inverse_factor(): pl.pallas_call(eliminate, out_shape=[pair, pair], in_specs=[pl.BlockSpec(...  3.78 us
  transfers between devices with their start and end apart: 6, of which 5 were waited for; matrix products, arithmetic and copies ran while one was open for 10% of the time, Pallas kernels for 3%

profile of v7, /device:TPU:1, one launch (start us, length us, event | category | flops | bytes accessed | tf_op | source)
XLA Modules:
  0.0 117.1 jit_solution(18298302868523612169)
XLA Ops:
  0.6 0.0 copy-start
  0.6 1.2 %copy-done = bf16[1,128,4096]{2,1,0:T(8,128)(2,1)S(1)} copy-done((bf16[1,128,4096]{2,1,0:T(8,128)(2,1)S(1)}, bf16[1,128,4096]{2,1,0:T(8,128)(2,1)}, u32[]{:S(2)}) %copy-start) | copy-done | bytes 1048600
  1.9 1.5 %convolution_convert_fusion.1 = bf16[128,64]{0,1:T(8,128)(2,1)S(1)} fusion(bf16[4096,64]{0,1:T(8,128)(2,1)} %param.7, bf16[1,128,4096]{2,1,0:T(8,128)(2,1)S(1)} %copy-done), kind=kOutput, calls=%fused_computation.6 | convolution fusion | flops 67117056 | bytes 1589248 | tf_op jit(solution)/shard_map/dot_general | solution.py:249
  3.4 0.8 broadcast_in_dim.6
  4.1 8.4 %all-to-all-start = ((bf16[16,64,128]{2,1,0:T(8,128)(2,1)}), bf16[16,64,128]{2,1,0:T(8,128)(2,1)S(1)}, u32[]{:S(2)}, u32[]{:S(2)}) async-start(bf16[16,64,128]{2,1,0:T(8,128)(2,1)} %broadcast_in_dim.6), calls=%async_computation | async-start | bytes 524288 | tf_op jit(solution)/shard_map/all_to_all | solution.py:28
  12.6 5.6 %fusion.2.base_ref = f32[64,896]{1,0:T(8,128)S(1)} fusion(bf16[4096,64]{0,1:T(8,128)(2,1)} %param.7, bf16[1,896,4096]{2,1,0:T(8,128)(2,1)} %param.6), kind=kOutput, calls=%fused_computation.2 | convolution fusion | flops 469762048 | bytes 8093696 | tf_op jit(solution)/shard_map/dot_general | solution.py:252
  18.2 3.1 %all-to-all-done.proj_ref = bf16[16,64,128]{2,1,0:T(8,128)(2,1)S(1)} async-done(((bf16[16,64,128]{2,1,0:T(8,128)(2,1)}), bf16[16,64,128]{2,1,0:T(8,128)(2,1)S(1)}, u32[]{:S(2)}, u32[]{:S(2)}) %all-to-all-start) | async-done | bytes 262176 | tf_op jit(solution)/shard_map/all_to_all | solution.py:28
  21.3 3.8 %left_terms.1 = (bf16[16,32,128]{2,1,0:T(8,128)(2,1)S(1)}, bf16[2048,896]{1,0:T(8,128)(2,1)}) custom-call(bf16[16,64,128]{2,1,0:T(8,128)(2,1)S(1)} %all-to-all-done.proj_ref, bf16[2048,896]{1,0:T(8,128)(2,1)} %bitcast.38, f32[64,896]{1,0:T(8,128)S(1)} %fusion.2.base_ref), custom_call_target="tpu_custom_call" | custom-call | flops 1000000000 | bytes 4194304 | tf_op jit(solution)/shard_map/left_terms/pallas_call | solution.py:108
  25.1 16.7 %all_to_all.35.parts_ref = bf16[16,32,128]{2,1,0:T(8,128)(2,1)S(1)} all-to-all(bf16[16,32,128]{2,1,0:T(8,128)(2,1)S(1)} %get-tuple-element.13), channel_id=1, replica_groups=mesh['z'=8,'ylo'=2,'yhi'=2,'x'=4,'core'=2] {'z','ylo'}, dimensions={0} | all-to-all | bytes 262144 | tf_op jit(solution)/shard_map/all_to_all | solution.py:28
  41.8 11.1 %all_to_all.36.parts_ref = bf16[16,32,128]{2,1,0:T(8,128)(2,1)S(1)} all-to-all(bf16[16,32,128]{2,1,0:T(8,128)(2,1)S(1)} %sum_copies.1), channel_id=1, replica_groups=mesh['z'=8,'ylo'=2,'yhi'=2,'x'=4,'core'=2] {'z','ylo'}, dimensions={0} | all-to-all | bytes 262144 | tf_op jit(solution)/shard_map/all_to_all | solution.py:28
  53.0 0.0 copy-start.1
  53.0 2.0 %copy-done.1 = bf16[2048,896]{1,0:T(8,128)(2,1)S(1)} copy-done((bf16[2048,896]{1,0:T(8,128)(2,1)S(1)}, bf16[2048,896]{1,0:T(8,128)(2,1)}, u32[]{:S(2)}) %copy-start.1) | copy-done | bytes 3670040
  55.0 2.0 %mixed_terms.1 = (bf16[16,72,128]{2,1,0:T(8,128)(2,1)}, bf16[64,896]{1,0:T(8,128)(2,1)S(1)}) custom-call(bf16[16,32,128]{2,1,0:T(8,128)(2,1)S(1)} %all_to_all.36.parts_ref, bf16[2048,896]{1,0:T(8,128)(2,1)S(1)} %copy-done.1), custom_call_target="tpu_custom_call" | custom-call | flops 1000000000 | bytes 4194304 | tf_op jit(solution)/shard_map/mixed_terms/pallas_call | solution.py:145
  57.0 7.7 %all-to-all-start.3 = ((bf16[16,72,128]{2,1,0:T(8,128)(2,1)}), bf16[16,72,128]{2,1,0:T(8,128)(2,1)S(1)}, u32[]{:S(2)}, u32[]{:S(2)}) async-start(bf16[16,72,128]{2,1,0:T(8,128)(2,1)} %get-tuple-element.17), calls=%async_computation.3 | async-start | bytes 589824 | tf_op jit(solution)/shard_map/all_to_all | solution.py:28
  64.7 4.5 %fusion = f32[64,4096]{1,0:T(8,128)S(1)} fusion(bf16[64,896]{1,0:T(8,128)(2,1)S(1)} %get-tuple-element.15, bf16[1,896,4096]{2,1,0:T(8,128)(2,1)} %param.6), kind=kOutput, calls=%fused_computation | convolution fusion | flops 469762048 | bytes 8503296 | tf_op jit(solution)/shard_map/dot_general | solution.py:24
  69.2 4.4 %all-to-all-done.3 = bf16[16,72,128]{2,1,0:T(8,128)(2,1)S(1)} async-done(((bf16[16,72,128]{2,1,0:T(8,128)(2,1)}), bf16[16,72,128]{2,1,0:T(8,128)(2,1)S(1)}, u32[]{:S(2)}, u32[]{:S(2)}) %all-to-all-start.3) | async-done | bytes 294944 | tf_op jit(solution)/shard_map/all_to_all | solution.py:28
  73.7 0.3 convolution_add_fusion
  74.0 0.1 select_convert_fusion
  74.0 1.0 collective-permute-start
  75.1 0.1 reduce-precision_convert_fusion
  75.1 0.1 fusion.13
  75.2 1.0 collective-permute-done
  76.2 0.1 bitcast_bitcast_fusion
  76.3 11.1 %all_to_all.37 = bf16[16,72,128]{2,1,0:T(8,128)(2,1)S(1)} all-to-all(bf16[16,72,128]{2,1,0:T(8,128)(2,1)S(1)} %pad_maximum_fusion), channel_id=1, replica_groups=mesh['z'=8,'ylo'=2,'yhi'=2,'x'=4,'core'=2] {'ylo','yhi','x'}, dimensions={0} | all-to-all | bytes 589824 | tf_op jit(solution)/shard_map/all_to_all | solution.py:28
  87.5 1.6 %collective-permute-start.1 = (bf16[8,8,128]{2,1,0:T(8,128)(2,1)S(1)}, bf16[8,8,128]{2,1,0:T(8,128)(2,1)S(1)}, u32[]{:S(2)}, u32[]{:S(2)}) collective-permute-start(bf16[8,8,128]{2,1,0:T(8,128)(2,1)S(1)} %slice.31), channel_id=1, source_target_pairs={{0,1},{1,0},{2,3},{3,2},{4,5},{5,4},{6,7},{7,6},{8,9},{9,8},{10,11... | collective-permute-start | bytes 49160 | tf_op jit(solution)/shard_map/ppermute | solution.py:37
  89.1 0.7 broadcast_in_dim.8
  89.7 3.4 %all-to-all-start.5 = ((bf16[8,64,128]{2,1,0:T(8,128)(2,1)}), bf16[8,64,128]{2,1,0:T(8,128)(2,1)S(1)}, u32[]{:S(2)}, u32[]{:S(2)}) async-start(bf16[8,64,128]{2,1,0:T(8,128)(2,1)} %broadcast_in_dim.8), calls=%async_computation.5 | async-start | bytes 262144 | tf_op jit(solution)/shard_map/all_to_all | solution.py:28
  93.1 0.0 collective-permute-done.1
  93.1 3.8 %inverse_factor.1 = (bf16[64,128]{1,0:T(8,128)(2,1)S(1)}, bf16[64,128]{1,0:T(8,128)(2,1)S(1)}) custom-call(bf16[8,8,128]{2,1,0:T(8,128)(2,1)S(1)} %get-tuple-element.25.zero_ref, bf16[8,8,128]{2,1,0:T(8,128)(2,1)S(1)} %get-tuple-element.24.one_ref), custom_call_target="tpu_custom_call" | custom-call | flops 4000000000 | bytes 49152 | tf_op jit(solution)/shard_map/inverse_factor/pallas_call | solution.py:202
  96.9 5.6 %all-to-all-done.5.parts_ref = bf16[8,64,128]{2,1,0:T(8,128)(2,1)S(1)} async-done(((bf16[8,64,128]{2,1,0:T(8,128)(2,1)}), bf16[8,64,128]{2,1,0:T(8,128)(2,1)S(1)}, u32[]{:S(2)}, u32[]{:S(2)}) %all-to-all-start.5) | async-done | bytes 131104 | tf_op jit(solution)/shard_map/all_to_all | solution.py:28
  102.5 0.2 scaled_copies.1
  102.7 10.8 %all_to_all.38 = bf16[16,64,128]{2,1,0:T(8,128)(2,1)S(1)} all-to-all(bf16[16,64,128]{2,1,0:T(8,128)(2,1)S(1)} %scaled_copies.1), channel_id=1, replica_groups=mesh['z'=8,'ylo'=2,'yhi'=2,'x'=4,'core'=2] {'ylo','yhi','x'}, dimensions={0} | all-to-all | bytes 524288 | tf_op jit(solution)/shard_map/all_to_all | solution.py:28
  113.5 1.6 %collective-permute-start.2 = (bf16[64,2048]{1,0:T(8,128)(2,1)S(1)}, bf16[64,2048]{1,0:T(8,128)(2,1)S(1)}, u32[]{:S(2)}, u32[]{:S(2)}) collective-permute-start(bf16[64,2048]{1,0:T(8,128)(2,1)S(1)} %copy_bitcast_fusion), channel_id=1, source_target_pairs={{0,1},{1,0},{2,3},{3,2},{4,5},{5,4},{6,7},{7,6},{8,9},{9,8},{10,11... | collective-permute-start | bytes 786440 | tf_op jit(solution)/shard_map/ppermute | solution.py:37
  115.0 0.8 convolution_convert_fusion
  115.8 0.3 collective-permute-done.2
  116.2 0.1 broadcast_select_fusion.1
  116.3 0.8 maximum_bitcast_fusion
  (9 shorter events, 0.2 us)
Async XLA Ops:
  0.6 1.2 %copy-start = (bf16[1,128,4096]{2,1,0:T(8,128)(2,1)S(1)}, bf16[1,128,4096]{2,1,0:T(8,128)(2,1)}, u32[]{:S(2)}) copy-start(bf16[1,128,4096]{2,1,0:T(8,128)(2,1)} %param.4) | copy-start | bytes 3145732
  4.1 17.1 %all-to-all-start = ((bf16[16,64,128]{2,1,0:T(8,128)(2,1)}), bf16[16,64,128]{2,1,0:T(8,128)(2,1)S(1)}, u32[]{:S(2)}, u32[]{:S(2)}) async-start(bf16[16,64,128]{2,1,0:T(8,128)(2,1)} %broadcast_in_dim.6), calls=%async_computation | async-start | bytes 524288 | tf_op jit(solution)/shard_map/all_to_all | solution.py:28
  53.0 2.0 %copy-start.1 = (bf16[2048,896]{1,0:T(8,128)(2,1)S(1)}, bf16[2048,896]{1,0:T(8,128)(2,1)}, u32[]{:S(2)}) copy-start(bf16[2048,896]{1,0:T(8,128)(2,1)} %get-tuple-element.14.h_ref) | copy-start | bytes 11010052
  57.0 16.6 %all-to-all-start.3 = ((bf16[16,72,128]{2,1,0:T(8,128)(2,1)}), bf16[16,72,128]{2,1,0:T(8,128)(2,1)S(1)}, u32[]{:S(2)}, u32[]{:S(2)}) async-start(bf16[16,72,128]{2,1,0:T(8,128)(2,1)} %get-tuple-element.17), calls=%async_computation.3 | async-start | bytes 589824 | tf_op jit(solution)/shard_map/all_to_all | solution.py:28
  74.0 2.2 %collective-permute-start = (bf16[64,2048]{1,0:T(8,128)(2,1)S(1)}, bf16[64,2048]{1,0:T(8,128)(2,1)S(1)}, u32[]{:S(2)}, u32[]{:S(2)}) collective-permute-start(bf16[64,2048]{1,0:T(8,128)(2,1)S(1)} %select_convert_fusion), channel_id=1, source_target_pairs={{0,1},{1,0},{2,3},{3,2},{4,5},{5,4},{6,7},{7,6},{8,9},{9,8},{10,11... | collective-permute-start | bytes 786440 | tf_op jit(solution)/shard_map/ppermute | solution.py:37
  87.5 5.6 %collective-permute-start.1 = (bf16[8,8,128]{2,1,0:T(8,128)(2,1)S(1)}, bf16[8,8,128]{2,1,0:T(8,128)(2,1)S(1)}, u32[]{:S(2)}, u32[]{:S(2)}) collective-permute-start(bf16[8,8,128]{2,1,0:T(8,128)(2,1)S(1)} %slice.31), channel_id=1, source_target_pairs={{0,1},{1,0},{2,3},{3,2},{4,5},{5,4},{6,7},{7,6},{8,9},{9,8},{10,11... | collective-permute-start | bytes 49160 | tf_op jit(solution)/shard_map/ppermute | solution.py:37
  89.7 12.8 %all-to-all-start.5 = ((bf16[8,64,128]{2,1,0:T(8,128)(2,1)}), bf16[8,64,128]{2,1,0:T(8,128)(2,1)S(1)}, u32[]{:S(2)}, u32[]{:S(2)}) async-start(bf16[8,64,128]{2,1,0:T(8,128)(2,1)} %broadcast_in_dim.8), calls=%async_computation.5 | async-start | bytes 262144 | tf_op jit(solution)/shard_map/all_to_all | solution.py:28
  113.5 2.7 %collective-permute-start.2 = (bf16[64,2048]{1,0:T(8,128)(2,1)S(1)}, bf16[64,2048]{1,0:T(8,128)(2,1)S(1)}, u32[]{:S(2)}, u32[]{:S(2)}) collective-permute-start(bf16[64,2048]{1,0:T(8,128)(2,1)S(1)} %copy_bitcast_fusion), channel_id=1, source_target_pairs={{0,1},{1,0},{2,3},{3,2},{4,5},{5,4},{6,7},{7,6},{8,9},{9,8},{10,11... | collective-permute-start | bytes 786440 | tf_op jit(solution)/shard_map/ppermute | solution.py:37

commit v8 on v5

--- a/solution.py
+++ b/solution.py
@@ -77,6 +77,22 @@
 
 def places(units):
     return [(r, c) for r in (0, ROWS) for c in range(0, units, LANES)]
+
+
+def hold_kernel(h_ref, held_ref):
+    held_ref[...] = h_ref[...]
+
+
+def hold(h_rows):
+    return pl.pallas_call(
+        hold_kernel,
+        out_shape=jax.ShapeDtypeStruct(h_rows.shape, h_rows.dtype),
+        in_specs=[pl.BlockSpec(memory_space=pltpu.VMEM)],
+        out_specs=pl.BlockSpec(memory_space=pltpu.VMEM),
+        cost_estimate=pl.CostEstimate(flops=0, bytes_accessed=8 << 20, transcendentals=0),
+        compiler_params=pltpu.CompilerParams(vmem_limit_bytes=3 * VMEM_BYTES),
+        name="hold",
+    )(h_rows)
 
 
 def left_kernel(proj_ref, h_ref, base_ref, out_ref):
@@ -228,9 +244,11 @@
     first, proj_local = lax.optimization_barrier((lax.axis_index("core") == 0, proj_local))
     proj = spread(proj_local.T, MP)
     base = jnp.dot(e_rows, q_prev, preferred_element_type=f32).T
-    p_terms = left_terms(proj, h_rows, base, groups)
+    base, h_rows = lax.optimization_barrier((base, h_rows))
+    h_held = hold(h_rows)
+    p_terms = left_terms(proj, h_held, base, groups)
     p_copies = sum_copies(exchange(p_terms, DP))
-    parts_of_mixed, p_sum = mixed_terms(exchange(p_copies, DP), h_rows, rank, units, parts)
+    parts_of_mixed, p_sum = mixed_terms(exchange(p_copies, DP), h_held, rank, units, parts)
     got = exchange(parts_of_mixed, MP)
     mixed = total(got[:, :rank]).astype(bf16)
     gram_rows = jnp.concatenate(halves(whole(total(got[:, rank : rank + some]))), axis=1)

time: 117 us -> 117 us (level)
  waiting for transfers between devices: 14.3 us -> 12.1 us
  starting transfers between devices: 23.7 us -> 25.9 us
    all_to_all x3, waiting for transfers between devices: 13 us -> 10.8 us  [exchange(): return lax.all_to_all(parts, axis, split_axis=0, concat_axis=0, tiled=True)]
    all_to_all x3, starting transfers between devices: 19.5 us -> 21.7 us  [exchange(): return lax.all_to_all(parts, axis, split_axis=0, concat_axis=0, tiled=True)]
    unnamed x6 -> x8, local copies, waits for them, and re-layouts: 5.29 us -> 5.04 us
where the time goes in v8:
time: 117 us; the launch traced here: 116 us
  blocking collectives  49.7 us (42%)
  starting transfers between devices  25.9 us (22%)
  matrix products  12.9 us (11%)
  waiting for transfers between devices  12.1 us (10%)
  Pallas kernels  7 us (6%)
  local copies, waits for them, and re-layouts  6.51 us (6%)
  other arithmetic  1.35 us (1%)
    all_to_all x4, blocking collectives, exchange(): return lax.all_to_all(parts, axis, split_axis=0, concat_axis=0, tiled=True)  49.7 us
    all_to_all x3, starting transfers between devices, exchange(): return lax.all_to_all(parts, axis, split_axis=0, concat_axis=0, tiled=True)  21.7 us
    all_to_all x3, waiting for transfers between devices, exchange(): return lax.all_to_all(parts, axis, split_axis=0, concat_axis=0, tiled=True)  10.8 us
    dot_general x1, matrix products, on_device(): base = jnp.dot(e_rows, q_prev, preferred_element_type=f32).T  5.74 us
    dot_general x3, matrix products, contract(): lax.dot_general(left, right, (dims, ((), ())), preferred_element_type=jnp...  5.62 us
    unnamed x8, local copies, waits for them, and re-layouts  5.04 us
    ppermute x3, starting transfers between devices, swap(): return lax.ppermute(block, 'core', [(0, 1), (1, 0)])  4.13 us
    pallas_call x1, Pallas kernels, inverse_factor(): pl.pallas_call(eliminate, out_shape=[pair, pair], in_specs=[pl.BlockSpec(...  3.78 us
  transfers between devices with their start and end apart: 6, of which 5 were waited for; matrix products, arithmetic and copies ran while one was open for 10% of the time, Pallas kernels for 3%

profile of v8, /device:TPU:1, one launch (start us, length us, event | category | flops | bytes accessed | tf_op | source)
XLA Modules:
  0.0 116.2 jit_solution(12087385007793008690)
XLA Ops:
  0.6 0.0 copy-start
  0.6 1.2 %copy-done = bf16[1,128,4096]{2,1,0:T(8,128)(2,1)S(1)} copy-done((bf16[1,128,4096]{2,1,0:T(8,128)(2,1)S(1)}, bf16[1,128,4096]{2,1,0:T(8,128)(2,1)}, u32[]{:S(2)}) %copy-start) | copy-done | bytes 1048600
  1.9 1.5 %convolution_convert_fusion.1 = bf16[128,64]{0,1:T(8,128)(2,1)S(1)} fusion(bf16[4096,64]{0,1:T(8,128)(2,1)} %param.7, bf16[1,128,4096]{2,1,0:T(8,128)(2,1)S(1)} %copy-done), kind=kOutput, calls=%fused_computation.6 | convolution fusion | flops 67117056 | bytes 1589248 | tf_op jit(solution)/shard_map/dot_general | solution.py:243
  3.4 0.8 broadcast_in_dim.6
  4.1 8.4 %all-to-all-start = ((bf16[16,64,128]{2,1,0:T(8,128)(2,1)}), bf16[16,64,128]{2,1,0:T(8,128)(2,1)S(1)}, u32[]{:S(2)}, u32[]{:S(2)}) async-start(bf16[16,64,128]{2,1,0:T(8,128)(2,1)} %broadcast_in_dim.6), calls=%async_computation | async-start | bytes 524288 | tf_op jit(solution)/shard_map/all_to_all | solution.py:27
  12.6 0.0 copy-start.3
  12.6 5.7 %fusion.2.base_ref = f32[64,896]{1,0:T(8,128)S(1)} fusion(bf16[4096,64]{0,1:T(8,128)(2,1)} %param.7, bf16[1,896,4096]{2,1,0:T(8,128)(2,1)} %param.6), kind=kOutput, calls=%fused_computation.2 | convolution fusion | flops 469762048 | bytes 8093696 | tf_op jit(solution)/shard_map/dot_general | solution.py:246
  18.3 0.0 copy-done.3
  18.4 0.3 hold.1.h_ref
  18.6 0.0 copy-start.1
  18.6 1.8 %copy-done.1 = bf16[2048,896]{1,0:T(8,128)(2,1)} copy-done((bf16[2048,896]{1,0:T(8,128)(2,1)}, bf16[2048,896]{1,0:T(8,128)(2,1)S(1)}, u32[]{:S(2)}) %copy-start.1) | copy-done | bytes 3670040
  20.4 0.8 all-to-all-done.proj_ref
  21.3 0.0 copy-start.2
  21.3 2.0 %copy-done.2 = bf16[2048,896]{1,0:T(8,128)(2,1)S(1)} copy-done((bf16[2048,896]{1,0:T(8,128)(2,1)S(1)}, bf16[2048,896]{1,0:T(8,128)(2,1)}, u32[]{:S(2)}) %copy-start.2) | copy-done | bytes 3670040
  23.3 0.7 left_terms.1
  24.0 16.7 %all_to_all.35.parts_ref = bf16[16,32,128]{2,1,0:T(8,128)(2,1)S(1)} all-to-all(bf16[16,32,128]{2,1,0:T(8,128)(2,1)S(1)} %left_terms.1), channel_id=1, replica_groups=mesh['z'=8,'ylo'=2,'yhi'=2,'x'=4,'core'=2] {'z','ylo'}, dimensions={0} | all-to-all | bytes 262144 | tf_op jit(solution)/shard_map/all_to_all | solution.py:27
  40.8 11.1 %all_to_all.36.parts_ref = bf16[16,32,128]{2,1,0:T(8,128)(2,1)S(1)} all-to-all(bf16[16,32,128]{2,1,0:T(8,128)(2,1)S(1)} %sum_copies.1), channel_id=1, replica_groups=mesh['z'=8,'ylo'=2,'yhi'=2,'x'=4,'core'=2] {'z','ylo'}, dimensions={0} | all-to-all | bytes 262144 | tf_op jit(solution)/shard_map/all_to_all | solution.py:27
  51.9 2.0 %mixed_terms.1 = (bf16[16,72,128]{2,1,0:T(8,128)(2,1)}, bf16[64,896]{1,0:T(8,128)(2,1)S(1)}) custom-call(bf16[16,32,128]{2,1,0:T(8,128)(2,1)S(1)} %all_to_all.36.parts_ref, bf16[2048,896]{1,0:T(8,128)(2,1)S(1)} %copy-done.2), custom_call_target="tpu_custom_call" | custom-call | flops 1000000000 | bytes 4194304 | tf_op jit(solution)/shard_map/mixed_terms/pallas_call | solution.py:139
  53.9 9.9 %all-to-all-start.3 = ((bf16[16,72,128]{2,1,0:T(8,128)(2,1)}), bf16[16,72,128]{2,1,0:T(8,128)(2,1)S(1)}, u32[]{:S(2)}, u32[]{:S(2)}) async-start(bf16[16,72,128]{2,1,0:T(8,128)(2,1)} %get-tuple-element.17), calls=%async_computation.3 | async-start | bytes 589824 | tf_op jit(solution)/shard_map/all_to_all | solution.py:27
  63.8 4.5 %fusion = f32[64,4096]{1,0:T(8,128)S(1)} fusion(bf16[64,896]{1,0:T(8,128)(2,1)S(1)} %get-tuple-element.15, bf16[1,896,4096]{2,1,0:T(8,128)(2,1)} %param.6), kind=kOutput, calls=%fused_computation | convolution fusion | flops 469762048 | bytes 8503296 | tf_op jit(solution)/shard_map/dot_general | solution.py:23
  68.3 4.4 %all-to-all-done.3 = bf16[16,72,128]{2,1,0:T(8,128)(2,1)S(1)} async-done(((bf16[16,72,128]{2,1,0:T(8,128)(2,1)}), bf16[16,72,128]{2,1,0:T(8,128)(2,1)S(1)}, u32[]{:S(2)}, u32[]{:S(2)}) %all-to-all-start.3) | async-done | bytes 294944 | tf_op jit(solution)/shard_map/all_to_all | solution.py:27
  72.8 0.3 convolution_add_fusion
  73.1 0.1 select_convert_fusion
  73.1 1.0 collective-permute-start
  74.2 0.1 reduce-precision_convert_fusion
  74.2 0.1 fusion.13
  74.3 1.0 collective-permute-done
  75.3 0.1 bitcast_bitcast_fusion
  75.4 11.1 %all_to_all.37 = bf16[16,72,128]{2,1,0:T(8,128)(2,1)S(1)} all-to-all(bf16[16,72,128]{2,1,0:T(8,128)(2,1)S(1)} %pad_maximum_fusion), channel_id=1, replica_groups=mesh['z'=8,'ylo'=2,'yhi'=2,'x'=4,'core'=2] {'ylo','yhi','x'}, dimensions={0} | all-to-all | bytes 589824 | tf_op jit(solution)/shard_map/all_to_all | solution.py:27
  86.6 1.6 %collective-permute-start.1 = (bf16[8,8,128]{2,1,0:T(8,128)(2,1)S(1)}, bf16[8,8,128]{2,1,0:T(8,128)(2,1)S(1)}, u32[]{:S(2)}, u32[]{:S(2)}) collective-permute-start(bf16[8,8,128]{2,1,0:T(8,128)(2,1)S(1)} %slice.31), channel_id=1, source_target_pairs={{0,1},{1,0},{2,3},{3,2},{4,5},{5,4},{6,7},{7,6},{8,9},{9,8},{10,11... | collective-permute-start | bytes 49160 | tf_op jit(solution)/shard_map/ppermute | solution.py:36
  88.2 0.7 broadcast_in_dim.8
  88.8 3.4 %all-to-all-start.5 = ((bf16[8,64,128]{2,1,0:T(8,128)(2,1)}), bf16[8,64,128]{2,1,0:T(8,128)(2,1)S(1)}, u32[]{:S(2)}, u32[]{:S(2)}) async-start(bf16[8,64,128]{2,1,0:T(8,128)(2,1)} %broadcast_in_dim.8), calls=%async_computation.5 | async-start | bytes 262144 | tf_op jit(solution)/shard_map/all_to_all | solution.py:27
  92.2 0.0 collective-permute-done.1
  92.2 3.8 %inverse_factor.1 = (bf16[64,128]{1,0:T(8,128)(2,1)S(1)}, bf16[64,128]{1,0:T(8,128)(2,1)S(1)}) custom-call(bf16[8,8,128]{2,1,0:T(8,128)(2,1)S(1)} %get-tuple-element.25.zero_ref, bf16[8,8,128]{2,1,0:T(8,128)(2,1)S(1)} %get-tuple-element.24.one_ref), custom_call_target="tpu_custom_call" | custom-call | flops 4000000000 | bytes 49152 | tf_op jit(solution)/shard_map/inverse_factor/pallas_call | solution.py:196
  96.0 5.6 %all-to-all-done.5.parts_ref = bf16[8,64,128]{2,1,0:T(8,128)(2,1)S(1)} async-done(((bf16[8,64,128]{2,1,0:T(8,128)(2,1)}), bf16[8,64,128]{2,1,0:T(8,128)(2,1)S(1)}, u32[]{:S(2)}, u32[]{:S(2)}) %all-to-all-start.5) | async-done | bytes 131104 | tf_op jit(solution)/shard_map/all_to_all | solution.py:27
  101.6 0.2 scaled_copies.1
  101.8 10.8 %all_to_all.38 = bf16[16,64,128]{2,1,0:T(8,128)(2,1)S(1)} all-to-all(bf16[16,64,128]{2,1,0:T(8,128)(2,1)S(1)} %scaled_copies.1), channel_id=1, replica_groups=mesh['z'=8,'ylo'=2,'yhi'=2,'x'=4,'core'=2] {'ylo','yhi','x'}, dimensions={0} | all-to-all | bytes 524288 | tf_op jit(solution)/shard_map/all_to_all | solution.py:27
  112.6 1.6 %collective-permute-start.2 = (bf16[64,2048]{1,0:T(8,128)(2,1)S(1)}, bf16[64,2048]{1,0:T(8,128)(2,1)S(1)}, u32[]{:S(2)}, u32[]{:S(2)}) collective-permute-start(bf16[64,2048]{1,0:T(8,128)(2,1)S(1)} %copy_bitcast_fusion), channel_id=1, source_target_pairs={{0,1},{1,0},{2,3},{3,2},{4,5},{5,4},{6,7},{7,6},{8,9},{9,8},{10,11... | collective-permute-start | bytes 786440 | tf_op jit(solution)/shard_map/ppermute | solution.py:36
  114.1 0.8 convolution_convert_fusion
  114.9 0.3 collective-permute-done.2
  115.3 0.1 broadcast_select_fusion.1
  115.4 0.8 maximum_bitcast_fusion
  (9 shorter events, 0.2 us)
Async XLA Ops:
  0.6 1.2 %copy-start = (bf16[1,128,4096]{2,1,0:T(8,128)(2,1)S(1)}, bf16[1,128,4096]{2,1,0:T(8,128)(2,1)}, u32[]{:S(2)}) copy-start(bf16[1,128,4096]{2,1,0:T(8,128)(2,1)} %param.4) | copy-start | bytes 3145732
  4.1 17.1 %all-to-all-start = ((bf16[16,64,128]{2,1,0:T(8,128)(2,1)}), bf16[16,64,128]{2,1,0:T(8,128)(2,1)S(1)}, u32[]{:S(2)}, u32[]{:S(2)}) async-start(bf16[16,64,128]{2,1,0:T(8,128)(2,1)} %broadcast_in_dim.6), calls=%async_computation | async-start | bytes 524288 | tf_op jit(solution)/shard_map/all_to_all | solution.py:27
  12.6 5.8 %copy-start.3 = (bf16[1,2048,896]{2,1,0:T(8,128)(2,1)S(1)}, bf16[1,2048,896]{2,1,0:T(8,128)(2,1)}, u32[]{:S(2)}) copy-start(bf16[1,2048,896]{2,1,0:T(8,128)(2,1)} %param.5) | copy-start | bytes 11010052
  18.6 1.8 %copy-start.1 = (bf16[2048,896]{1,0:T(8,128)(2,1)}, bf16[2048,896]{1,0:T(8,128)(2,1)S(1)}, u32[]{:S(2)}) copy-start(bf16[2048,896]{1,0:T(8,128)(2,1)S(1)} %hold.1.h_ref) | copy-start | bytes 11010052
  21.3 2.0 %copy-start.2 = (bf16[2048,896]{1,0:T(8,128)(2,1)S(1)}, bf16[2048,896]{1,0:T(8,128)(2,1)}, u32[]{:S(2)}) copy-start(bf16[2048,896]{1,0:T(8,128)(2,1)} %copy-done.1) | copy-start | bytes 11010052
  53.9 18.8 %all-to-all-start.3 = ((bf16[16,72,128]{2,1,0:T(8,128)(2,1)}), bf16[16,72,128]{2,1,0:T(8,128)(2,1)S(1)}, u32[]{:S(2)}, u32[]{:S(2)}) async-start(bf16[16,72,128]{2,1,0:T(8,128)(2,1)} %get-tuple-element.17), calls=%async_computation.3 | async-start | bytes 589824 | tf_op jit(solution)/shard_map/all_to_all | solution.py:27
  73.1 2.2 %collective-permute-start = (bf16[64,2048]{1,0:T(8,128)(2,1)S(1)}, bf16[64,2048]{1,0:T(8,128)(2,1)S(1)}, u32[]{:S(2)}, u32[]{:S(2)}) collective-permute-start(bf16[64,2048]{1,0:T(8,128)(2,1)S(1)} %select_convert_fusion), channel_id=1, source_target_pairs={{0,1},{1,0},{2,3},{3,2},{4,5},{5,4},{6,7},{7,6},{8,9},{9,8},{10,11... | collective-permute-start | bytes 786440 | tf_op jit(solution)/shard_map/ppermute | solution.py:36
  86.6 5.6 %collective-permute-start.1 = (bf16[8,8,128]{2,1,0:T(8,128)(2,1)S(1)}, bf16[8,8,128]{2,1,0:T(8,128)(2,1)S(1)}, u32[]{:S(2)}, u32[]{:S(2)}) collective-permute-start(bf16[8,8,128]{2,1,0:T(8,128)(2,1)S(1)} %slice.31), channel_id=1, source_target_pairs={{0,1},{1,0},{2,3},{3,2},{4,5},{5,4},{6,7},{7,6},{8,9},{9,8},{10,11... | collective-permute-start | bytes 49160 | tf_op jit(solution)/shard_map/ppermute | solution.py:36
  88.8 12.8 %all-to-all-start.5 = ((bf16[8,64,128]{2,1,0:T(8,128)(2,1)}), bf16[8,64,128]{2,1,0:T(8,128)(2,1)S(1)}, u32[]{:S(2)}, u32[]{:S(2)}) async-start(bf16[8,64,128]{2,1,0:T(8,128)(2,1)} %broadcast_in_dim.8), calls=%async_computation.5 | async-start | bytes 262144 | tf_op jit(solution)/shard_map/all_to_all | solution.py:27
  112.6 2.7 %collective-permute-start.2 = (bf16[64,2048]{1,0:T(8,128)(2,1)S(1)}, bf16[64,2048]{1,0:T(8,128)(2,1)S(1)}, u32[]{:S(2)}, u32[]{:S(2)}) collective-permute-start(bf16[64,2048]{1,0:T(8,128)(2,1)S(1)} %copy_bitcast_fusion), channel_id=1, source_target_pairs={{0,1},{1,0},{2,3},{3,2},{4,5},{5,4},{6,7},{7,6},{8,9},{9,8},{10,11... | collective-permute-start | bytes 786440 | tf_op jit(solution)/shard_map/ppermute | solution.py:36
